TPU v7x, 32 devices: a whole 2x2x4 slice. The times are simulated.
32 devices in a mesh: gx: 4 (over y, x), gy: 8 (over z, core).
Axes of the slice: x: 2, y: 2, z: 4, core: 2. Of those that a mesh axis runs over, the one named last changes fastest.
Arguments:
- features: bfloat16 [16, 128, 128, 128], P(None, 'gx', 'gy'), may hold values from -24 to 24
- w_first: bfloat16 [27, 16, 16], replicated, may hold values from -0.3125 to 0.3125
- w_second: bfloat16 [27, 16, 16], replicated, may hold values from -0.3125 to 0.3125
- w_lift: bfloat16 [512, 16], replicated, may hold values from -1.5 to 1.5
- w_coarse: bfloat16 [512, 27, 512], P('gy'), may hold values from -0.0546875 to 0.0546875
- w_decode: bfloat16 [16, 512], replicated, may hold values from -0.25 to 0.25
- w_joining: bfloat16 [16, 32], replicated, may hold values from -1 to 1
Outputs:
- joined: bfloat16 [16, 128, 128, 128], P(None, 'gx', 'gy')
All inputs are finite; a program needn't handle non-finite values.
Results may differ from a plain program's by a relative error of at most 0.0065.
Values may be sent and summed in bfloat16 or wider, within the bound.
A program may use at most 192 MiB of HBM per device.

v0:
```python
import jax
import jax.numpy as jnp
from jax import lax
from jax.sharding import PartitionSpec as P

POOL = 16


def extended_2(x, sides, width):
    for axis, dim in sides:
        count, length = (lax.axis_size(axis), x.shape[dim])
        up = [(i, (i + 1) % count) for i in range(count - 1)]
        down = [(j, i) for i, j in up]
        last = lax.slice_in_dim(x, length - width, length, axis=dim)
        leading = lax.slice_in_dim(x, 0, width, axis=dim)
        before = lax.ppermute(last, axis, up)
        after = lax.ppermute(leading, axis, down)
        x = jnp.concatenate([before, x, after], axis=dim)
    return x


def conv_block(padded, weight, out_x, out_y):
    count = weight.shape[1]
    inner = weight.shape[2]
    extended = jnp.pad(padded, ((0, 0), (0, 0), (0, 0), (1, 1)))
    depth = extended.shape[3] - 2
    total = jnp.zeros((count, out_x, out_y, depth), jnp.float32)
    for shift_a in range(3):
        slabs = []
        for shift_b in range(3):
            for shift_c in range(3):
                slabs.append(
                    extended[
                        :,
                        shift_a : shift_a + out_x,
                        shift_b : shift_b + out_y,
                        shift_c : shift_c + depth,
                    ]
                )
        stacked = jnp.concatenate(slabs, axis=0)
        matrix = jnp.transpose(weight[9 * shift_a : 9 * shift_a + 9], (1, 0, 2)).reshape(
            count, 9 * inner
        )
        total = total + jnp.einsum(
            "ok,kxyz->oxyz", matrix, stacked, preferred_element_type=jnp.float32
        )
    return total


def coarse_conv(padded, weight, out_x, out_y, out_z):
    total = jnp.zeros((weight.shape[0], out_x, out_y, out_z), jnp.float32)
    for offset in range(27):
        shift_a, shift_b, shift_c = (offset // 9, offset // 3 % 3, offset % 3)
        window = padded[
            :, shift_a : shift_a + out_x, shift_b : shift_b + out_y, shift_c : shift_c + out_z
        ]
        total = total + jnp.einsum(
            "oc,cxyz->oxyz", weight[:, offset, :], window, preferred_element_type=jnp.float32
        )
    return total


def lift_cells(lift_float, pooled_cells):
    raised = jnp.einsum("oc,cxyz->oxyz", lift_float, pooled_cells, precision=lax.Precision.HIGHEST)
    return jnp.maximum(raised, 0.0).astype(jnp.bfloat16)


def local(features, w_first, w_second, w_lift, w_coarse, w_decode, w_joining):
    chans, size_x, size_y, depth = features.shape
    along_x = lax.axis_size("gx")
    along_y = lax.axis_size("gy")
    block_x, block_y, block_z = (size_x // POOL, size_y // POOL, depth // POOL)
    cells = block_x * block_y * block_z
    padded = extended_2(features, (("gx", 1), ("gy", 2)), 2)
    raw = jnp.maximum(conv_block(padded, w_first, size_x + 2, size_y + 2), 0.0)
    global_x = lax.axis_index("gx") * size_x + jnp.arange(size_x + 2) - 1
    global_y = lax.axis_index("gy") * size_y + jnp.arange(size_y + 2) - 1
    inside_x = (global_x >= 0) & (global_x < size_x * along_x)
    inside_y = (global_y >= 0) & (global_y < size_y * along_y)
    inside = inside_x[:, None] & inside_y[None, :]
    first = jnp.where(inside[None, :, :, None], raw, 0.0).astype(jnp.bfloat16)
    second = jnp.maximum(conv_block(first, w_second, size_x, size_y), 0.0).astype(jnp.bfloat16)
    blocks = second.reshape(chans, block_x, POOL, block_y, POOL, block_z, POOL)
    pooled = jnp.sum(blocks, axis=(2, 4, 6), dtype=jnp.float32) / float(POOL**3)
    lift_float = w_lift.astype(jnp.float32)
    rim = extended_2(pooled, (("gx", 1), ("gy", 2)), 1)
    rim = jnp.pad(rim, ((0, 0), (0, 0), (0, 0), (1, 1)))
    lifted_pad = lift_cells(lift_float, rim)
    piece = lax.all_gather(w_coarse, "gy", axis=0, tiled=True)
    total = coarse_conv(lifted_pad, piece, block_x, block_y, block_z)
    coarse = jnp.maximum(total, 0.0).astype(jnp.bfloat16).reshape(piece.shape[0], cells)
    decoded = jnp.dot(w_decode, coarse, preferred_element_type=jnp.float32).astype(jnp.bfloat16)
    decoded = decoded.reshape(chans, block_x, block_y, block_z)
    up_term = jnp.einsum(
        "oc,cxyz->oxyz", w_joining[:, chans:], decoded, preferred_element_type=jnp.float32
    )
    skip_term = jnp.einsum(
        "oc,cxyz->oxyz", w_joining[:, :chans], second, preferred_element_type=jnp.float32
    )
    skip_term = skip_term.reshape(chans, block_x, POOL, block_y, POOL, block_z, POOL)
    joined = skip_term + up_term[:, :, None, :, None, :, None]
    return joined.reshape(chans, size_x, size_y, depth).astype(jnp.bfloat16)


def solution(mesh):
    in_specs = (P(None, "gx", "gy", None), P(), P(), P(), P("gy", None, None), P(), P())
    out_specs = P(None, "gx", "gy", None)
    return jax.shard_map(local, mesh=mesh, in_specs=in_specs, out_specs=out_specs, check_vma=False)
```

profile of v0, /device:TPU:11, one launch (start us, length us, event | category | flops | bytes accessed | tf_op | source)
XLA Modules:
  0.0 269.5 jit_solution(14409597603138350803)
XLA Ops:
  8.3 3.1 %collective-permute-start = (bf16[16,2,16,128]{3,0,2,1:T(8,128)(2,1)S(1)}, bf16[16,2,16,128]{3,0,2,1:T(8,128)(2,1)S(1)}, u32[]{:S(2)}, u32[]{:S(2)}) collective-permute-start(bf16[16,2,16,128]{3,0,2,1:T(8,128)(2,1)S(1)} %copy.86), channel_id=1, source_target_pairs={{0,8},{8,16},{16,24},{1,9},{9,17},{17,25},{2,10},{10,18},{18,26},{... | collective-permute-start | bytes 393224 | tf_op jit(solution)/shard_map/ppermute | solution.py:16
  11.5 2.2 collective-permute-start.1
  17.0 4.4 %constant_dynamic-update-slice_fusion.1 = bf16[16,36,16,128]{3,0,2,1:T(8,128)(2,1)S(1)} fusion(bf16[16,36,16,128]{3,0,2,1:T(8,128)(2,1)S(1)} %constant_dynamic-update-slice_fusion.2, bf16[16,32,16,128]{3,2,1,0:T(8,128)(2,1)} %param.7), kind=kLoop, calls=%fused_computation.185 | loop fusion | bytes 4194304
  21.5 4.4 %collective-permute-start.2 = (bf16[16,36,2,128]{3,0,2,1:T(8,128)(2,1)S(1)}, bf16[16,36,2,128]{3,0,2,1:T(8,128)(2,1)S(1)}, u32[]{:S(2)}, u32[]{:S(2)}) collective-permute-start(bf16[16,36,2,128]{3,0,2,1:T(8,128)(2,1)S(1)} %get-tuple-element.23), channel_id=1, source_target_pairs={{0,1},{1,2},{2,3},{3,4},{4,5},{5,6},{6,7},{8,9},{9,10},{10,11},{11... | collective-permute-start | bytes 884744 | tf_op jit(solution)/shard_map/ppermute | solution.py:16
  25.9 2.2 collective-permute-start.3
  28.2 12.4 %collective-permute-done.2 = bf16[16,36,2,128]{3,0,2,1:T(8,128)(2,1)S(1)} collective-permute-done((bf16[16,36,2,128]{3,0,2,1:T(8,128)(2,1)S(1)}, bf16[16,36,2,128]{3,0,2,1:T(8,128)(2,1)S(1)}, u32[]{:S(2)}, u32[]{:S(2)}) %collective-permute-start.2) | collective-permute-done | bytes 294944 | tf_op jit(solution)/shard_map/ppermute | solution.py:16
  40.6 4.6 %collective-permute-done.3 = bf16[16,36,2,128]{3,0,2,1:T(8,128)(2,1)S(1)} collective-permute-done((bf16[16,36,2,128]{3,0,2,1:T(8,128)(2,1)S(1)}, bf16[16,36,2,128]{3,0,2,1:T(8,128)(2,1)S(1)}, u32[]{:S(2)}, u32[]{:S(2)}) %collective-permute-start.3) | collective-permute-done | bytes 294944 | tf_op jit(solution)/shard_map/ppermute | solution.py:17
  51.7 3.5 %fusion.26 = (bf16[144,34,18,128]{3,0,2,1:T(8,128)(2,1)S(1)}, bf16[144,34,18,128]{3,0,2,1:T(8,128)(2,1)}) fusion(bf16[144,34,18,128]{3,0,2,1:T(8,128)(2,1)S(1)} %fusion.25, bf16[16,36,20,128]{3,0,2,1:T(8,128)(2,1)S(1)} %pad_maximum_fusion), kind=kLoop, calls=%fused_computation.71 | loop fusion | bytes 7962624
  55.2 2.5 fusion.28
  57.6 5.2 %fusion.27 = (bf16[144,34,18,128]{3,0,2,1:T(8,128)(2,1)S(1)}, bf16[144,34,18,128]{3,0,2,1:T(8,128)(2,1)}, bf16[144,34,18,128]{3,0,2,1:T(8,128)(2,1)}) fusion(bf16[144,34,18,128]{3,0,2,1:T(8,128)(2,1)S(1)} %get-tuple-element.21, bf16[16,36,20,128]{3,0,2,1:T(8,128)(2,1)S(1)} %pad_maximum_fusion, bf16[144,34,18,128]{3,0,2,1:T(8,128)(2,1)} %get-tuple-element.22), kind=kLoop, calls=%fused_computation.72 | loop fusion | bytes 10469376 | tf_op jit(solution)/shard_map/concatenate | solution.py:40
  62.9 2.3 fusion.6
  65.2 3.0 %fusion.17 = bf16[144,34,18,128]{3,0,2,1:T(8,128)(2,1)} fusion(bf16[144,34,18,128]{3,0,2,1:T(8,128)(2,1)} %fusion.6, bf16[16,36,20,128]{3,0,2,1:T(8,128)(2,1)S(1)} %pad_maximum_fusion), kind=kLoop, calls=%fused_computation.62 | loop fusion | bytes 5455872
  68.1 3.2 %fusion.18 = bf16[144,34,18,128]{3,0,2,1:T(8,128)(2,1)} fusion(bf16[144,34,18,128]{3,0,2,1:T(8,128)(2,1)} %fusion.17, bf16[16,36,20,128]{3,0,2,1:T(8,128)(2,1)S(1)} %pad_maximum_fusion), kind=kLoop, calls=%fused_computation.63 | loop fusion | bytes 5455872
  71.3 2.3 slice_dynamic-update-slice_fusion.1
  73.6 2.3 fusion.19
  75.9 2.3 fusion.20
  78.2 2.0 fusion.2
  80.2 4.0 %fusion.21 = (bf16[144,34,18,128]{3,0,2,1:T(8,128)(2,1)}, bf16[144,34,18,128]{3,0,2,1:T(8,128)(2,1)}) fusion(bf16[144,34,18,128]{3,0,2,1:T(8,128)(2,1)} %fusion.2, bf16[16,36,20,128]{3,0,2,1:T(8,128)(2,1)S(1)} %pad_maximum_fusion, bf16[144,34,18,128]{3,0,2,1:T(8,128)(2,1)} %get-tuple-element.6), kind=kLoop, calls=%fused_computation.66 | loop fusion | bytes 7962624 | tf_op jit(solution)/shard_map/concatenate | solution.py:40
  84.3 1.9 slice_dynamic-update-slice_fusion.2
  86.2 2.3 fusion.13
  88.5 2.3 fusion.14
  90.9 2.0 fusion.4
  92.8 2.4 fusion.15
  95.2 11.8 %fusion.92 = f32[34,18,128,16]{2,3,1,0:T(8,128)} fusion(bf16[144,34,18,128]{3,0,2,1:T(8,128)(2,1)} %fusion.15, bf16[16,144,1,1]{0,1,3,2:T(8,128)(2,1)S(1)} %bitcast.335), kind=kOutput, calls=%fused_computation.253 | convolution fusion | flops 360972288 | bytes 27578880 | tf_op jit(solution)/shard_map/ok,kxyz->oxyz/dot_general | solution.py:44
  107.1 5.0 %fusion.93 = f32[34,18,128,16]{2,3,1,0:T(8,128)} fusion(bf16[144,34,18,128]{3,0,2,1:T(8,128)(2,1)S(1)} %bitcast.329, bf16[16,144,1,1]{0,1,3,2:T(8,128)(2,1)S(1)} %bitcast.334), kind=kOutput, calls=%fused_computation.254 | convolution fusion | flops 360972288 | bytes 27578880 | tf_op jit(solution)/shard_map/ok,kxyz->oxyz/dot_general | solution.py:44
  112.1 12.2 %fusion.9 = bf16[16,34,18,128]{3,0,2,1:T(8,128)(2,1)S(1)} fusion(f32[34,18,128,16]{2,3,1,0:T(8,128)} %fusion.92, f32[34,18,128,16]{2,3,1,0:T(8,128)} %fusion.93, pred[34,18]{1,0:T(8,128)(4,1)S(1)} %broadcast_and_fusion, bf16[144,34,18,128]{3,0,2,1:T(8,128)(2,1)} %copy-done.2, bf16[16,144,1,1]{0,1,3,2:T(8,128)(2,1)S(1)} %bitcast.333), kind=kOutput, calls=%fused_computation.54 | convolution fusion | flops 367239168 | bytes 35099748 | tf_op jit(solution)/shard_map/ok,kxyz->oxyz/dot_general | solution.py:44
  130.0 3.1 %fusion.46 = (bf16[144,32,16,128]{3,0,2,1:T(8,128)(2,1)S(1)}, bf16[144,32,16,128]{3,0,2,1:T(8,128)(2,1)}) fusion(bf16[144,32,16,128]{3,0,2,1:T(8,128)(2,1)S(1)} %fusion.45, bf16[16,34,18,128]{3,0,2,1:T(8,128)(2,1)S(1)} %fusion.9), kind=kLoop, calls=%fused_computation.96 | loop fusion | bytes 6701056
  133.1 2.7 %slice_dynamic-update-slice_fusion.3 = (bf16[144,32,16,128]{3,0,2,1:T(8,128)(2,1)S(1)}, bf16[144,32,16,128]{3,0,2,1:T(8,128)(2,1)}) fusion(bf16[144,32,16,128]{3,0,2,1:T(8,128)(2,1)S(1)} %get-tuple-element.17, bf16[16,34,18,128]{3,0,2,1:T(8,128)(2,1)S(1)} %fusion.9, bf16[144,32,16,128]{3,0,2,1:T(8,128)(2,1)} %get-tuple-element.18), kind=kLoop, calls=%fused_computation.98 | loop fusion | bytes 8388608
  135.8 4.3 %fusion.47 = (bf16[144,32,16,128]{3,0,2,1:T(8,128)(2,1)S(1)}, bf16[144,32,16,128]{3,0,2,1:T(8,128)(2,1)}, bf16[144,32,16,128]{3,0,2,1:T(8,128)(2,1)}) fusion(bf16[144,32,16,128]{3,0,2,1:T(8,128)(2,1)S(1)} %get-tuple-element.15, bf16[16,34,18,128]{3,0,2,1:T(8,128)(2,1)S(1)} %fusion.9, bf16[144,32,16,128]{3,0,2,1:T(8,128)(2,1)} %get-tuple-element.16), kind=kLoop, calls=%fused_computation.97 | loop fusion | bytes 8798208 | tf_op jit(solution)/shard_map/concatenate | solution.py:40
  140.1 2.4 slice_dynamic-update-slice_fusion.8
  142.5 2.8 %fusion.37 = bf16[144,32,16,128]{3,0,2,1:T(8,128)(2,1)} fusion(bf16[144,32,16,128]{3,0,2,1:T(8,128)(2,1)} %slice_dynamic-update-slice_fusion.8, bf16[16,34,18,128]{3,0,2,1:T(8,128)(2,1)S(1)} %fusion.9), kind=kLoop, calls=%fused_computation.87 | loop fusion | bytes 4603904
  145.3 2.9 %fusion.38 = bf16[144,32,16,128]{3,0,2,1:T(8,128)(2,1)} fusion(bf16[144,32,16,128]{3,0,2,1:T(8,128)(2,1)} %fusion.37, bf16[16,34,18,128]{3,0,2,1:T(8,128)(2,1)S(1)} %fusion.9), kind=kLoop, calls=%fused_computation.88 | loop fusion | bytes 4603904
  148.1 2.0 slice_dynamic-update-slice_fusion.7
  150.1 2.1 fusion.39
  152.2 2.0 fusion.40
  154.2 2.0 slice_dynamic-update-slice_fusion.6
  156.2 3.5 %fusion.41 = (bf16[144,32,16,128]{3,0,2,1:T(8,128)(2,1)}, bf16[144,32,16,128]{3,0,2,1:T(8,128)(2,1)}) fusion(bf16[144,32,16,128]{3,0,2,1:T(8,128)(2,1)} %slice_dynamic-update-slice_fusion.6, bf16[16,34,18,128]{3,0,2,1:T(8,128)(2,1)S(1)} %fusion.9, bf16[144,32,16,128]{3,0,2,1:T(8,128)(2,1)} %get-tuple-element.13), kind=kLoop, calls=%fused_computation.91 | loop fusion | bytes 6701056 | tf_op jit(solution)/shard_map/concatenate | solution.py:40
  159.7 2.0 slice_dynamic-update-slice_fusion.10
  161.7 2.0 fusion.33
  163.8 2.0 fusion.34
  165.8 2.2 slice_dynamic-update-slice_fusion.9
  168.0 2.0 fusion.35
  170.0 7.8 %fusion.94 = f32[32,16,128,16]{2,3,1,0:T(8,128)S(1)} fusion(bf16[144,32,16,128]{3,0,2,1:T(8,128)(2,1)} %fusion.35, bf16[16,144,1,1]{0,1,3,2:T(8,128)(2,1)S(1)} %bitcast.332), kind=kOutput, calls=%fused_computation.255 | convolution fusion | flops 301989888 | bytes 23073280 | tf_op jit(solution)/shard_map/ok,kxyz->oxyz/dot_general | solution.py:44
  177.8 8.0 %fusion.95 = f32[32,16,128,16]{2,3,1,0:T(8,128)S(1)} fusion(bf16[144,32,16,128]{3,0,2,1:T(8,128)(2,1)} %get-tuple-element.19, bf16[16,144,1,1]{0,1,3,2:T(8,128)(2,1)S(1)} %bitcast.331), kind=kOutput, calls=%fused_computation.256 | convolution fusion | flops 301989888 | bytes 23073280 | tf_op jit(solution)/shard_map/ok,kxyz->oxyz/dot_general | solution.py:44
  185.8 9.3 %convert_reduce_fusion = (f32[16,32,128]{2,0,1:T(8,128)S(1)}, bf16[32,16,128,16]{2,3,1,0:T(8,128)(2,1)S(1)}) fusion(bf16[144,32,16,128]{3,0,2,1:T(8,128)(2,1)} %copy-done.1, bf16[16,144,1,1]{0,1,3,2:T(8,128)(2,1)S(1)} %bitcast.330, f32[32,16,128,16]{2,3,1,0:T(8,128)S(1)} %fusion.94, f32[32,16,128,16]{2,3,1,0:T(8,128)S(1)} %fusion.95), kind=kOutput, calls=%fused_computation.39 | convolution fusion | flops 308215808 | bytes 29626880 | tf_op jit(solution)/shard_map/ok,kxyz->oxyz/dot_general | solution.py:44
  195.1 1.9 reduce_sum.14
  197.0 1.8 reduce_sum.18
  198.9 8.8 %collective-permute-start.4 = (f32[16,1,1,8]{0,3,2,1:T(8,128)S(1)}, f32[16,1,1,8]{0,3,2,1:T(8,128)S(1)}, u32[]{:S(2)}, u32[]{:S(2)}) collective-permute-start(f32[16,1,1,8]{0,3,2,1:T(8,128)S(1)} %get-tuple-element.33), channel_id=1, source_target_pairs={{0,8},{8,16},{16,24},{1,9},{9,17},{17,25},{2,10},{10,18},{18,26},{... | collective-permute-start | bytes 1544 | tf_op jit(solution)/shard_map/ppermute | solution.py:16
  207.7 1.9 collective-permute-start.5
  209.6 3.3 %collective-permute-done.5 = f32[16,1,1,8]{0,3,2,1:T(8,128)S(1)} collective-permute-done((f32[16,1,1,8]{0,3,2,1:T(8,128)S(1)}, f32[16,1,1,8]{0,3,2,1:T(8,128)S(1)}, u32[]{:S(2)}, u32[]{:S(2)}) %collective-permute-start.5) | collective-permute-done | bytes 544 | tf_op jit(solution)/shard_map/ppermute | solution.py:17
  213.0 2.4 collective-permute-start.6
  215.4 1.9 collective-permute-start.7
  217.3 3.1 %collective-permute-done.7 = f32[16,4,1,8]{0,3,2,1:T(8,128)S(1)} collective-permute-done((f32[16,4,1,8]{0,3,2,1:T(8,128)S(1)}, f32[16,4,1,8]{0,3,2,1:T(8,128)S(1)}, u32[]{:S(2)}, u32[]{:S(2)}) %collective-permute-start.7) | collective-permute-done | bytes 2080 | tf_op jit(solution)/shard_map/ppermute | solution.py:17
  222.0 1.3 convolution_add_fusion.15
  224.6 1.3 convolution_add_fusion.13
  225.9 1.3 convolution_add_fusion.12
  227.2 1.3 convolution_add_fusion.11
  228.5 1.3 convolution_add_fusion.10
  229.8 1.3 convolution_add_fusion.9
  231.1 1.3 convolution_add_fusion.8
  254.4 1.4 fusion.65
  256.1 1.6 add.212
  257.7 2.2 add.213
  260.6 1.9 copy.70
  (87 shorter events, 43.4 us)
Async XLA Ops:
  6.5 213.9 %copy-start = (bf16[512,16]{0,1:T(8,128)(2,1)S(1)}, bf16[512,16]{0,1:T(8,128)(2,1)}, u32[]{:S(2)}) copy-start(bf16[512,16]{0,1:T(8,128)(2,1)} %param.10) | copy-start | bytes 49156
  6.5 214.2 %all-gather.2.cloned.1.call-start = ((), (), s32[]{:S(2)}) async-start(), calls=%async_computation | async-start | bytes 15925248 | tf_op jit(solution)/shard_map/all_gather | solution.py:89
  8.3 8.7 %collective-permute-start = (bf16[16,2,16,128]{3,0,2,1:T(8,128)(2,1)S(1)}, bf16[16,2,16,128]{3,0,2,1:T(8,128)(2,1)S(1)}, u32[]{:S(2)}, u32[]{:S(2)}) collective-permute-start(bf16[16,2,16,128]{3,0,2,1:T(8,128)(2,1)S(1)} %copy.86), channel_id=1, source_target_pairs={{0,8},{8,16},{16,24},{1,9},{9,17},{17,25},{2,10},{10,18},{18,26},{... | collective-permute-start | bytes 393224 | tf_op jit(solution)/shard_map/ppermute | solution.py:16
  11.5 9.9 %collective-permute-start.1 = (bf16[16,2,16,128]{3,0,2,1:T(8,128)(2,1)S(1)}, bf16[16,2,16,128]{3,0,2,1:T(8,128)(2,1)S(1)}, u32[]{:S(2)}, u32[]{:S(2)}) collective-permute-start(bf16[16,2,16,128]{3,0,2,1:T(8,128)(2,1)S(1)} %copy.87), channel_id=1, source_target_pairs={{8,0},{16,8},{24,16},{9,1},{17,9},{25,17},{10,2},{18,10},{26,18},{... | collective-permute-start | bytes 393224 | tf_op jit(solution)/shard_map/ppermute | solution.py:17
  21.5 19.0 %collective-permute-start.2 = (bf16[16,36,2,128]{3,0,2,1:T(8,128)(2,1)S(1)}, bf16[16,36,2,128]{3,0,2,1:T(8,128)(2,1)S(1)}, u32[]{:S(2)}, u32[]{:S(2)}) collective-permute-start(bf16[16,36,2,128]{3,0,2,1:T(8,128)(2,1)S(1)} %get-tuple-element.23), channel_id=1, source_target_pairs={{0,1},{1,2},{2,3},{3,4},{4,5},{5,6},{6,7},{8,9},{9,10},{10,11},{11... | collective-permute-start | bytes 884744 | tf_op jit(solution)/shard_map/ppermute | solution.py:16
  25.9 19.3 %collective-permute-start.3 = (bf16[16,36,2,128]{3,0,2,1:T(8,128)(2,1)S(1)}, bf16[16,36,2,128]{3,0,2,1:T(8,128)(2,1)S(1)}, u32[]{:S(2)}, u32[]{:S(2)}) collective-permute-start(bf16[16,36,2,128]{3,0,2,1:T(8,128)(2,1)S(1)} %get-tuple-element.24), channel_id=1, source_target_pairs={{1,0},{2,1},{3,2},{4,3},{5,4},{6,5},{7,6},{9,8},{10,9},{11,10},{12... | collective-permute-start | bytes 884744 | tf_op jit(solution)/shard_map/ppermute | solution.py:17
  62.8 15.4 %copy-start.2 = (bf16[144,34,18,128]{3,0,2,1:T(8,128)(2,1)}, bf16[144,34,18,128]{3,0,2,1:T(8,128)(2,1)S(1)}, u32[]{:S(2)}) copy-start(bf16[144,34,18,128]{3,0,2,1:T(8,128)(2,1)S(1)} %get-tuple-element.5) | copy-start | bytes 67682304
  88.5 18.5 %slice-start = ((s8[22560768]{0:T(1024)(128)(4,1)}), s8[4194304]{0:T(1024)(128)(4,1)S(1)}, s32[]{:S(2)}) async-start(s8[22560768]{0:T(1024)(128)(4,1)} %bitcast.328), calls=%async_computation.1 | async-start | bytes 8388608
  90.8 16.2 %slice-start.1 = ((s8[22560768]{0:T(1024)(128)(4,1)}), s8[4194304]{0:T(1024)(128)(4,1)S(1)}, s32[]{:S(2)}) async-start(s8[22560768]{0:T(1024)(128)(4,1)} %bitcast.328), calls=%async_computation.2 | async-start | bytes 8388608
  92.8 14.2 %slice-start.2 = ((s8[22560768]{0:T(1024)(128)(4,1)}), s8[4194304]{0:T(1024)(128)(4,1)S(1)}, s32[]{:S(2)}) async-start(s8[22560768]{0:T(1024)(128)(4,1)} %bitcast.328), calls=%async_computation.3 | async-start | bytes 8388608
  95.2 11.9 %slice-start.3 = ((s8[22560768]{0:T(1024)(128)(4,1)}), s8[4194304]{0:T(1024)(128)(4,1)S(1)}, s32[]{:S(2)}) async-start(s8[22560768]{0:T(1024)(128)(4,1)} %bitcast.328), calls=%async_computation.4 | async-start | bytes 8388608
  95.2 11.9 %slice-start.4 = ((s8[22560768]{0:T(1024)(128)(4,1)}), s8[4194304]{0:T(1024)(128)(4,1)S(1)}, s32[]{:S(2)}) async-start(s8[22560768]{0:T(1024)(128)(4,1)} %bitcast.328), calls=%async_computation.5 | async-start | bytes 8388608
  95.2 11.9 %slice-start.5 = ((s8[22560768]{0:T(1024)(128)(4,1)}), s8[1589248]{0:T(1024)(128)(4,1)S(1)}, s32[]{:S(2)}) async-start(s8[22560768]{0:T(1024)(128)(4,1)} %bitcast.328), calls=%async_computation.6 | async-start | bytes 3178496
  140.1 16.2 %copy-start.1 = (bf16[144,32,16,128]{3,0,2,1:T(8,128)(2,1)}, bf16[144,32,16,128]{3,0,2,1:T(8,128)(2,1)S(1)}, u32[]{:S(2)}) copy-start(bf16[144,32,16,128]{3,0,2,1:T(8,128)(2,1)S(1)} %get-tuple-element.12) | copy-start | bytes 56623108
  195.1 59.3 %copy-start.4 = (bf16[16,512]{1,0:T(8,128)(2,1)S(1)}, bf16[16,512]{1,0:T(8,128)(2,1)}, u32[]{:S(2)}) copy-start(bf16[16,512]{1,0:T(8,128)(2,1)} %param.12) | copy-start | bytes 49156
  195.1 60.7 %copy-start.3 = (bf16[16,32]{1,0:T(8,128)(2,1)S(1)}, bf16[16,32]{1,0:T(8,128)(2,1)}, u32[]{:S(2)}) copy-start(bf16[16,32]{1,0:T(8,128)(2,1)} %param.13) | copy-start | bytes 3076
  198.9 10.7 %collective-permute-start.4 = (f32[16,1,1,8]{0,3,2,1:T(8,128)S(1)}, f32[16,1,1,8]{0,3,2,1:T(8,128)S(1)}, u32[]{:S(2)}, u32[]{:S(2)}) collective-permute-start(f32[16,1,1,8]{0,3,2,1:T(8,128)S(1)} %get-tuple-element.33), channel_id=1, source_target_pairs={{0,8},{8,16},{16,24},{1,9},{9,17},{17,25},{2,10},{10,18},{18,26},{... | collective-permute-start | bytes 1544 | tf_op jit(solution)/shard_map/ppermute | solution.py:16
  207.7 5.3 %collective-permute-start.5 = (f32[16,1,1,8]{0,3,2,1:T(8,128)S(1)}, f32[16,1,1,8]{0,3,2,1:T(8,128)S(1)}, u32[]{:S(2)}, u32[]{:S(2)}) collective-permute-start(f32[16,1,1,8]{0,3,2,1:T(8,128)S(1)} %get-tuple-element.34), channel_id=1, source_target_pairs={{8,0},{16,8},{24,16},{9,1},{17,9},{25,17},{10,2},{18,10},{26,18},{... | collective-permute-start | bytes 1544 | tf_op jit(solution)/shard_map/ppermute | solution.py:17
  213.0 4.3 %collective-permute-start.6 = (f32[16,4,1,8]{0,3,2,1:T(8,128)S(1)}, f32[16,4,1,8]{0,3,2,1:T(8,128)S(1)}, u32[]{:S(2)}, u32[]{:S(2)}) collective-permute-start(f32[16,4,1,8]{0,3,2,1:T(8,128)S(1)} %pad_maximum_fusion.3), channel_id=1, source_target_pairs={{0,1},{1,2},{2,3},{3,4},{4,5},{5,6},{6,7},{8,9},{9,10},{10,11},{11... | collective-permute-start | bytes 6152 | tf_op jit(solution)/shard_map/ppermute | solution.py:16
  215.4 5.1 %collective-permute-start.7 = (f32[16,4,1,8]{0,3,2,1:T(8,128)S(1)}, f32[16,4,1,8]{0,3,2,1:T(8,128)S(1)}, u32[]{:S(2)}, u32[]{:S(2)}) collective-permute-start(f32[16,4,1,8]{0,3,2,1:T(8,128)S(1)} %pad_maximum_fusion.3), channel_id=1, source_target_pairs={{1,0},{2,1},{3,2},{4,3},{5,4},{6,5},{7,6},{9,8},{10,9},{11,10},{12... | collective-permute-start | bytes 6152 | tf_op jit(solution)/shard_map/ppermute | solution.py:17
Sparse Core Ops, SparseCore 0:
  9.0 131.5 all-gather.1
where the time goes:
time: 275 us; the launch traced here: 270 us
  local copies, waits for them, and re-layouts  102 us (37%)
  matrix products  90.3 us (33%)
  starting transfers between devices  26.9 us (10%)
  waiting for transfers between devices  24.1 us (9%)
  between operations  14.1 us (5%)
  other arithmetic  12 us (4%)
    unnamed x59, local copies, waits for them, and re-layouts  68.7 us
    dot_general x6, matrix products, conv_block(): jnp.einsum('ok,kxyz->oxyz', matrix, stacked, preferred_element_type=jnp.f...  54.1 us
    dot_general x26, matrix products, coarse_conv(): jnp.einsum('oc,cxyz->oxyz', weight[:, offset, :], window, preferred_eleme...  33.6 us
    concatenate x6, local copies, waits for them, and re-layouts, conv_block(): stacked = jnp.concatenate(slabs, axis=0)  21.4 us
    ppermute x4, starting transfers between devices, extended_2(): before = lax.ppermute(last, axis, up)  18.7 us
    ppermute x4, waiting for transfers between devices, extended_2(): before = lax.ppermute(last, axis, up)  12.4 us
    ppermute x4, waiting for transfers between devices, extended_2(): after = lax.ppermute(leading, axis, down)  11 us
    unnamed x6, other arithmetic  9.68 us
  transfers between devices with their start and end apart: 9, of which 4 were waited for; matrix products, arithmetic and copies ran while one was open for 60% of the time, Pallas kernels for 0%

commit v1 on v0

v1 whole, which is shorter than its diff:
```python
import jax
import jax.numpy as jnp
import numpy as np
from jax import lax
from jax.experimental import pallas as pl
from jax.experimental.pallas import tpu as pltpu
from jax.sharding import PartitionSpec as P

POOL = 16
FAR = 4096
VMEM_LIMIT = 48 * 1024 * 1024


def rows_of(chans, size_y, width):
    own_c = np.repeat(np.arange(chans), size_y)
    own_y = np.tile(np.arange(size_y), chans)
    side_y = list(range(-width, 0)) + list(range(size_y, size_y + width))
    rim_c = np.tile(np.arange(chans), len(side_y))
    rim_y = np.repeat(np.array(side_y, dtype=np.int64), chans)
    return np.concatenate([own_c, rim_c]), np.concatenate([own_y, rim_y])


def spread_maps(chans, size_y, out_width, in_width):
    out_c, out_y = rows_of(chans, size_y, out_width)
    in_c, in_y = rows_of(chans, size_y, in_width)
    rows, cols = len(out_c), len(in_c)
    left = np.zeros((3 * rows, 3 * chans), np.float32)
    right = np.zeros((3 * chans, 3 * cols), np.float32)
    for tap in range(3):
        left[tap * rows + np.arange(rows), tap * chans + out_c] = 1.0
        right[tap * chans + in_c, tap * cols + np.arange(cols)] = 1.0
    as_bf = lambda v: jnp.asarray(v, jnp.bfloat16)
    return (
        as_bf(left),
        as_bf(right),
        jnp.asarray(np.tile(out_y, 3)[:, None], jnp.int32),
        jnp.asarray(np.tile(in_y, 3)[None, :], jnp.int32),
    )


def build_matrix(weight_ref, left_ref, right_ref, out_y_ref, in_y_ref, matrix_ref):
    gap = in_y_ref[...] - out_y_ref[...]
    total = jnp.zeros(matrix_ref.shape, jnp.float32)
    for shift_b in range(3):
        part = jnp.dot(left_ref[...], weight_ref[shift_b], preferred_element_type=jnp.float32)
        part = jnp.dot(
            part.astype(jnp.bfloat16), right_ref[...], preferred_element_type=jnp.float32
        )
        total = jnp.where(gap == shift_b - 1, part, total)
    matrix_ref[...] = total.astype(jnp.bfloat16)


def shift_sum(parts, rows, group, depth):
    lane = lax.broadcasted_iota(jnp.int32, (rows, depth), 1)
    planes = []
    for plane in range(group):
        cut = parts[:, plane * depth : (plane + 1) * depth]
        before = jnp.where(lane == 0, 0.0, pltpu.roll(cut[:rows], 1, 1))
        after = jnp.where(lane == depth - 1, 0.0, pltpu.roll(cut[2 * rows :], depth - 1, 1))
        planes.append(before + cut[rows : 2 * rows] + after)
    return planes


def stack_planes(planes, group):
    return jnp.concatenate(
        [jnp.concatenate(planes[a : a + group], axis=1) for a in range(3)], axis=0
    )


def fine_kernel(
    own_ref, rim_ref, w1_ref, w2_ref, l1, r1, oy1, iy1, l2, r2, oy2, iy2, edge_ref, cells_ref,
    lanes_ref, second_ref, pooled_ref, m1_ref, m2_ref, first_ref, sums_ref,
):
    chans, planes_in, size_y, depth = own_ref.shape
    size_x = second_ref.shape[0]
    group = 2
    build_matrix(w1_ref, l1, r1, oy1, iy1, m1_ref)
    build_matrix(w2_ref, l2, r2, oy2, iy2, m2_ref)
    rows1 = first_ref.shape[1]
    rows2 = second_ref.shape[1]

    def one(step, carry):
        at = step * group
        planes = []
        for k in range(group + 2):
            own = own_ref[:, at + k].reshape(chans * size_y, depth)
            planes.append(jnp.concatenate([own, rim_ref[at + k]], axis=0))
        data = stack_planes(planes, group)
        parts = jnp.dot(m1_ref[...], data, preferred_element_type=jnp.float32)
        sums = shift_sum(parts, rows1, group, depth)
        for k in range(group):
            first_ref[at + k] = jnp.maximum(sums[k], 0.0).astype(jnp.bfloat16)
        return carry

    lax.fori_loop(0, (size_x + 2) // group, one, 0)
    first_ref[0] = first_ref[0] * edge_ref[0:1, :].astype(jnp.bfloat16)
    first_ref[size_x + 1] = first_ref[size_x + 1] * edge_ref[1:2, :].astype(jnp.bfloat16)
    sums_ref[...] = jnp.zeros_like(sums_ref)

    def two(step, carry):
        at = step * group
        data = stack_planes([first_ref[at + k] for k in range(group + 2)], group)
        parts = jnp.dot(m2_ref[...], data, preferred_element_type=jnp.float32)
        sums = shift_sum(parts, rows2, group, depth)
        total = None
        for k in range(group):
            value = jnp.maximum(sums[k], 0.0).astype(jnp.bfloat16)
            second_ref[at + k] = value
            value = value.astype(jnp.float32)
            total = value if total is None else total + value
        block = at // POOL
        sums_ref[block] = sums_ref[block] + total
        return carry

    lax.fori_loop(0, size_x // group, two, 0)
    for block in range(size_x // POOL):
        by_row = jnp.dot(
            cells_ref[...], sums_ref[block],
            precision=lax.Precision.HIGHEST, preferred_element_type=jnp.float32,
        )
        pooled_ref[block] = jnp.dot(
            by_row, lanes_ref[...],
            precision=lax.Precision.HIGHEST, preferred_element_type=jnp.float32,
        ) / float(POOL**3)


def fine(own, rim, w_first, w_second, size_x):
    chans, _, size_y, depth = own.shape
    along_x, along_y = lax.axis_size("gx"), lax.axis_size("gy")
    at_x, at_y = lax.axis_index("gx"), lax.axis_index("gy")
    l1, r1, oy1, iy1 = spread_maps(chans, size_y, 1, 2)
    l2, r2, oy2, iy2 = spread_maps(chans, size_y, 0, 1)
    beyond = ((at_y == 0) & (oy1 < 0)) | ((at_y == along_y - 1) & (oy1 >= size_y))
    oy1 = jnp.where(beyond, FAR, oy1)

    def by_offset(weight):
        taps = weight.reshape(3, 3, 3, chans, chans)
        return jnp.transpose(taps, (1, 2, 3, 0, 4)).reshape(3, 3 * chans, 3 * chans)

    edge = jnp.stack([at_x > 0, at_x < along_x - 1]).astype(jnp.float32)
    edge = jnp.broadcast_to(edge[:, None], (2, depth))
    cells = jnp.asarray(np.repeat(np.eye(chans, dtype=np.float32), size_y, axis=1))
    lanes = jnp.asarray(np.repeat(np.eye(depth // POOL, dtype=np.float32), POOL, axis=0))
    rows1, rows2 = l1.shape[0] // 3, l2.shape[0] // 3
    cols1, cols2 = r1.shape[1], r2.shape[1]
    spec = pl.BlockSpec(memory_space=pltpu.VMEM)
    flops = 2 * depth * (3 * rows1 * cols1 * (size_x + 2) + 3 * rows2 * cols2 * size_x)
    return pl.pallas_call(
        fine_kernel,
        out_shape=(
            jax.ShapeDtypeStruct((size_x, rows2, depth), jnp.bfloat16),
            jax.ShapeDtypeStruct((size_x // POOL, chans, depth // POOL), jnp.float32),
        ),
        in_specs=[spec] * 15,
        out_specs=(spec, spec),
        scratch_shapes=[
            pltpu.VMEM((3 * rows1, cols1), jnp.bfloat16),
            pltpu.VMEM((3 * rows2, cols2), jnp.bfloat16),
            pltpu.VMEM((size_x + 2, rows1, depth), jnp.bfloat16),
            pltpu.VMEM((size_x // POOL, rows2, depth), jnp.float32),
        ],
        compiler_params=pltpu.CompilerParams(vmem_limit_bytes=VMEM_LIMIT),
        cost_estimate=pl.CostEstimate(flops=flops, bytes_accessed=8_000_000, transcendentals=0),
        name="fine",
    )(
        own, rim, by_offset(w_first), by_offset(w_second),
        l1, r1, oy1, iy1, l2, r2, oy2, iy2, edge, cells, lanes,
    )


def join_kernel(second_ref, up_ref, matrix_ref, out_ref):
    planes, rows, depth = second_ref.shape
    chans, _, size_y, _ = out_ref.shape
    up = up_ref[0]
    up = jnp.concatenate([up] * 2, axis=1)
    for at in range(0, planes, 2):
        data = jnp.concatenate([second_ref[at], second_ref[at + 1]], axis=1)
        skip = jnp.dot(matrix_ref[...], data, preferred_element_type=jnp.float32)
        value = (skip + up).astype(jnp.bfloat16)
        for k in range(2):
            cut = value[:, k * depth : (k + 1) * depth]
            out_ref[:, at + k] = cut.reshape(chans, size_y, depth)


def join(second, up, w_skip):
    size_x, rows, depth = second.shape
    chans = w_skip.shape[0]
    size_y = rows // chans
    up = jnp.repeat(jnp.repeat(up, POOL, axis=2), size_y, axis=1)
    matrix = w_skip[:, None, :, None] * jnp.eye(size_y, dtype=w_skip.dtype)[None, :, None, :]
    matrix = matrix.reshape(rows, rows)
    step = 8
    return pl.pallas_call(
        join_kernel,
        grid=(size_x // step,),
        out_shape=jax.ShapeDtypeStruct((chans, size_x, size_y, depth), jnp.bfloat16),
        in_specs=[
            pl.BlockSpec((step, rows, depth), lambda i: (i, 0, 0)),
            pl.BlockSpec((1, rows, depth), lambda i: (i * step // POOL, 0, 0)),
            pl.BlockSpec((rows, rows), lambda i: (0, 0)),
        ],
        out_specs=pl.BlockSpec((chans, step, size_y, depth), lambda i: (0, i, 0, 0)),
        compiler_params=pltpu.CompilerParams(vmem_limit_bytes=VMEM_LIMIT),
        cost_estimate=pl.CostEstimate(
            flops=2 * size_x * rows * rows * depth, bytes_accessed=5_000_000, transcendentals=0
        ),
        name="join",
    )(second, up, matrix)


def halo(features):
    chans, size_x, size_y, depth = features.shape
    nx, ny = lax.axis_size("gx"), lax.axis_size("gy")

    def both(axis, count, last, leading):
        up = [(i, i + 1) for i in range(count - 1)]
        down = [(j, i) for i, j in up]
        return lax.ppermute(last, axis, up), lax.ppermute(leading, axis, down)

    before, after = both("gx", nx, features[:, size_x - 2 :], features[:, :2])
    own = jnp.concatenate([before, features, after], axis=1)

    def side(v):
        return jnp.transpose(v, (1, 2, 0, 3)).reshape(size_x + 4, 2 * chans, depth)

    below, above = both("gy", ny, side(own[:, :, size_y - 2 :]), side(own[:, :, :2]))
    return own, jnp.concatenate([below, above], axis=1)


def coarse_level(pooled, w_lift, w_coarse, w_decode):
    block_x, chans, block_z = pooled.shape
    nx, ny = lax.axis_size("gx"), lax.axis_size("gy")
    at_x, at_y = lax.axis_index("gx"), lax.axis_index("gy")
    every = lax.all_gather(pooled, ("gx", "gy"), axis=0)
    every = every.reshape(nx, ny, block_x, chans, block_z)
    every = jnp.transpose(every, (0, 2, 1, 4, 3)).reshape(nx * block_x, ny, block_z, chans)
    every = jnp.pad(every, ((1, 1), (1, 1), (1, 1), (0, 0)))
    near = lax.dynamic_slice_in_dim(every, at_x * block_x, block_x + 2, axis=0)
    raised = jnp.einsum(
        "xyzc,oc->xyzo", near, w_lift.astype(jnp.float32), precision=lax.Precision.HIGHEST
    )
    lifted = jnp.maximum(raised, 0.0).astype(jnp.bfloat16)
    windows = []
    for offset in range(27):
        a, b, c = offset // 9, offset // 3 % 3, offset % 3
        cut = lifted[a : a + block_x, b : b + ny, c : c + block_z]
        windows.append(cut.reshape(block_x * ny * block_z, -1))
    stacked = jnp.concatenate(windows, axis=1)
    count = w_coarse.shape[0]
    total = lax.dot_general(
        stacked, w_coarse.reshape(count, -1), (((1,), (1,)), ((), ())),
        preferred_element_type=jnp.float32,
    )
    coarse = jnp.maximum(total, 0.0).astype(jnp.bfloat16)
    mine = lax.dynamic_slice_in_dim(w_decode, at_y * count, count, axis=1)
    part = lax.dot_general(
        coarse, mine, (((1,), (1,)), ((), ())), preferred_element_type=jnp.float32
    )
    part = jnp.transpose(part.reshape(block_x, ny, block_z, chans), (1, 0, 3, 2))
    whole = lax.psum_scatter(part, "gy", scatter_dimension=0, tiled=False)
    return whole.astype(jnp.bfloat16)


def local(features, w_first, w_second, w_lift, w_coarse, w_decode, w_joining):
    chans, size_x, size_y, depth = features.shape
    own, rim = halo(features)
    second, pooled = fine(own, rim, w_first, w_second, size_x)
    decoded = coarse_level(pooled, w_lift, w_coarse, w_decode)
    up = jnp.einsum(
        "oc,xcz->xoz", w_joining[:, chans:], decoded, preferred_element_type=jnp.float32
    )
    return join(second, up, w_joining[:, :chans])


def solution(mesh):
    in_specs = (P(None, "gx", "gy", None), P(), P(), P(), P("gy", None, None), P(), P())
    out_specs = P(None, "gx", "gy", None)
    return jax.shard_map(local, mesh=mesh, in_specs=in_specs, out_specs=out_specs, check_vma=False)
```

time: 275 us -> 150 us (0.55)
  the two profiles are of different devices: /device:TPU:11 before, /device:TPU:0 now
where the time goes in v1:
time: 150 us
  blocking collectives  68 us (45%)
  Pallas kernels  30.7 us (20%)
  local copies, waits for them, and re-layouts  29.1 us (19%)
  starting transfers between devices  11.2 us (7%)
  matrix products  5.45 us (4%)
  waiting for transfers between devices  3.08 us (2%)
  other arithmetic  2.13 us (1%)
    all_gather x1, blocking collectives, coarse_level(): every = lax.all_gather(pooled, ('gx', 'gy'), axis=0)  41.4 us
    pallas_call x1, Pallas kernels, fine(): pl.pallas_call(fine_kernel, out_shape=(jax.ShapeDtypeStruct((size_x, rows...  28.1 us
    unnamed x1, blocking collectives  26.6 us
    unnamed x67, local copies, waits for them, and re-layouts  21 us
    ppermute x4, starting transfers between devices, both(): return (lax.ppermute(last, axis, up), lax.ppermute(leading, axis, down))  11.2 us
    dot_general x1, matrix products, coarse_level(): lax.dot_general(coarse, mine, (((1,), (1,)), ((), ())), preferred_element...  4.01 us
    ppermute x4, waiting for transfers between devices, both(): return (lax.ppermute(last, axis, up), lax.ppermute(leading, axis, down))  3.08 us
  transfers between devices with their start and end apart: 4, of which 2 were waited for; matrix products, arithmetic and copies ran while one was open for 6% of the time, Pallas kernels for 0%

profile of v1, /device:TPU:0, one launch (start us, length us, event | category | flops | bytes accessed | tf_op | source)
XLA Modules:
  0.0 150.0 jit_solution(15612831618965648240)
XLA Ops:
  0.0 1.0 fusion.16
  1.0 4.8 %collective-permute-start = (bf16[16,2,16,128]{3,2,1,0:T(8,128)(2,1)S(1)}, bf16[16,2,16,128]{3,2,1,0:T(8,128)(2,1)S(1)}, u32[]{:S(2)}, u32[]{:S(2)}) collective-permute-start(bf16[16,2,16,128]{3,2,1,0:T(8,128)(2,1)S(1)} %get-tuple-element.12), channel_id=1, source_target_pairs={{0,8},{8,16},{16,24},{1,9},{9,17},{17,25},{2,10},{10,18},{18,26},{... | collective-permute-start | bytes 393224 | tf_op jit(solution)/shard_map/ppermute | solution.py:218
  5.9 1.3 collective-permute-start.1
  7.2 0.8 broadcast_multiply_fusion
  8.0 0.6 collective-permute-done
  8.6 2.2 %constant_dynamic-update-slice_fusion.1 = bf16[16,36,16,128]{3,2,1,0:T(8,128)(2,1)S(1)} fusion(bf16[16,36,16,128]{3,2,1,0:T(8,128)(2,1)S(1)} %constant_dynamic-update-slice_fusion.2, bf16[16,32,16,128]{3,2,1,0:T(8,128)(2,1)} %param.17), kind=kLoop, calls=%fused_computation.13 | loop fusion | bytes 4194304
  10.8 2.5 %collective-permute-done.1 = bf16[16,2,16,128]{3,2,1,0:T(8,128)(2,1)S(1)} collective-permute-done((bf16[16,2,16,128]{3,2,1,0:T(8,128)(2,1)S(1)}, bf16[16,2,16,128]{3,2,1,0:T(8,128)(2,1)S(1)}, u32[]{:S(2)}, u32[]{:S(2)}) %collective-permute-start.1) | collective-permute-done | bytes 131104 | tf_op jit(solution)/shard_map/ppermute | solution.py:218
  13.4 0.5 slice_bitcast_fusion.1
  13.9 0.8 copy.36
  14.7 1.3 collective-permute-start.3
  16.0 3.7 %collective-permute-start.2 = (bf16[36,32,128]{2,1,0:T(8,128)(2,1)S(1)}, bf16[36,32,128]{2,1,0:T(8,128)(2,1)}, u32[]{:S(2)}, u32[]{:S(2)}) collective-permute-start(bf16[36,32,128]{2,1,0:T(8,128)(2,1)S(1)} %bitcast.110), channel_id=1, source_target_pairs={{0,1},{1,2},{2,3},{3,4},{4,5},{5,6},{6,7},{8,9},{9,10},{10,11},{11... | collective-permute-start | bytes 884744 | tf_op jit(solution)/shard_map/ppermute | solution.py:218
  19.8 0.1 add_convert_fusion
  19.8 0.2 copy.37
  20.0 0.1 copy.38
  20.1 0.1 reshape.151.w1_ref
  20.2 0.2 copy.39
  20.4 0.1 copy.40
  20.5 0.1 reshape.153.w2_ref
  20.8 2.9 %copy.50 = bf16[27,8,8,512]{3,2,0,1:T(8,128)(2,1)} copy(bf16[27,8,8,512]{3,2,1,0:T(8,128)(2,1)} %bitcast.78) | data formatting | bytes 3538944 | tf_op jit(solution)/shard_map/reshape | solution.py:251
  23.7 1.0 mul.28.matrix_ref
  24.7 0.6 dynamic-slice
  25.3 0.1 or_select_fusion.oy1
  25.4 1.1 pad_maximum_fusion.rim_ref
  26.5 0.1 broadcast_in_dim.19.edge_ref
  26.7 28.1 %fine.1 = (bf16[32,256,128]{2,1,0:T(8,128)(2,1)S(1)}, f32[2,16,8]{2,1,0:T(8,128)S(1)}) custom-call(bf16[16,36,16,128]{3,2,1,0:T(8,128)(2,1)} %copy-done.11, bf16[36,64,128]{2,1,0:T(8,128)(2,1)S(1)} %pad_maximum_fusion.rim_ref, bf16[3,48,48]{2,1,0:T(8,128)(2,1)S(1)} %reshape.151.w1_ref, bf16[3,48,48]{2,1,0:T(8,128)(2,1)S(1)} %reshape.153.w2_ref, ...), custom_call_target="tpu_custom_call" | custom-call | flops 12655263744 | bytes 8000000 | tf_op jit(solution)/shard_map/fine/pallas_call | solution.py:148
  54.8 0.1 copy.41
  54.9 41.4 %all-gather = f32[64,16,8]{1,2,0:T(8,128)S(1)} all-gather(f32[2,16,8]{1,2,0:T(8,128)S(1)} %copy.41), channel_id=2, replica_groups=mesh['gx'=4,'gy'=8] {'gx','gy'}, dimensions={0}, use_global_device_ids=true | all-gather | bytes 33792 | tf_op jit(solution)/shard_map/all_gather | solution.py:234
  96.3 0.6 fusion
  96.9 0.1 fusion.18
  97.1 0.3 fusion.17
  97.4 0.7 constant_dynamic-update-slice_fusion.29
  98.1 0.7 constant_dynamic-update-slice_fusion.28
  98.7 0.7 constant_dynamic-update-slice_fusion.27
  99.4 0.7 constant_dynamic-update-slice_fusion.26
  100.1 0.7 constant_dynamic-update-slice_fusion.25
  100.8 0.7 constant_dynamic-update-slice_fusion.24
  101.5 0.7 constant_dynamic-update-slice_fusion.23
  102.1 0.7 constant_dynamic-update-slice_fusion.22
  102.8 0.7 constant_dynamic-update-slice_fusion.21
  103.5 0.7 constant_dynamic-update-slice_fusion.20
  104.2 0.7 constant_dynamic-update-slice_fusion.19
  104.9 0.7 constant_dynamic-update-slice_fusion.18
  105.5 0.7 constant_dynamic-update-slice_fusion.17
  106.2 0.7 constant_dynamic-update-slice_fusion.16
  106.9 0.7 constant_dynamic-update-slice_fusion.15
  107.6 0.7 constant_dynamic-update-slice_fusion.14
  108.2 0.7 constant_dynamic-update-slice_fusion.13
  108.9 0.7 constant_dynamic-update-slice_fusion.12
  109.6 0.7 constant_dynamic-update-slice_fusion.11
  110.3 0.7 constant_dynamic-update-slice_fusion.10
  111.0 0.7 constant_dynamic-update-slice_fusion.9
  111.7 0.7 constant_dynamic-update-slice_fusion.8
  112.4 0.7 constant_dynamic-update-slice_fusion.7
  113.0 0.7 constant_dynamic-update-slice_fusion.6
  113.7 0.7 constant_dynamic-update-slice_fusion.5
  114.4 0.7 constant_dynamic-update-slice_fusion.4
  115.0 0.7 constant_dynamic-update-slice_fusion.3
  115.7 4.0 %fusion.2 = f32[128,16]{1,0:T(8,128)S(1)} fusion(bf16[128,13824]{1,0:T(8,128)(2,1)} %constant_dynamic-update-slice_fusion.3, bf16[64,13824]{1,0:T(8,128)(2,1)} %bitcast.77, bf16[16,512]{1,0:T(8,128)(2,1)} %param.22, s32[]{:T(128)S(6)} %select_n.12), kind=kOutput, calls=%fused_computation.4 | convolution fusion | flops 226770944 | bytes 5320708 | tf_op jit(solution)/shard_map/dot_general | solution.py:256
  119.7 26.6 %all-reduce.1 = bf16[8,2,16,8]{2,3,0,1:T(8,128)(2,1)S(1)} all-reduce(f32[8,2,16,8]{2,3,0,1:T(8,128)S(1)} %bitcast.111), channel_id=3, replica_groups=mesh['gx'=4,'gy'=8] {'gy'}, use_global_device_ids=true, to_apply=%region_0.1.clone | all-reduce | flops 2048 | bytes 12288
  146.3 0.8 convolution_bitcast_fusion
  147.1 0.1 copy.45
  147.2 0.1 broadcast_in_dim.20
  147.3 0.1 reshape.185
  147.4 2.6 %join.1 = bf16[16,32,16,128]{3,2,1,0:T(8,128)(2,1)} custom-call(bf16[32,256,128]{2,1,0:T(8,128)(2,1)S(1)} %get-tuple-element.7.second_ref, f32[2,256,128]{2,1,0:T(8,128)S(1)} %bitcast.76, bf16[256,256]{1,0:T(8,128)(2,1)S(1)} %mul.28.matrix_ref), custom_call_target="tpu_custom_call" | custom-call | flops 536870912 | bytes 5000000 | tf_op jit(solution)/shard_map/join/pallas_call | solution.py:193
  (44 shorter events, 0.2 us)
Async XLA Ops:
  0.0 96.3 %copy-start = (bf16[512,16]{0,1:T(8,128)(2,1)S(1)}, bf16[512,16]{0,1:T(8,128)(2,1)}, u32[]{:S(2)}) copy-start(bf16[512,16]{0,1:T(8,128)(2,1)} %param.20) | copy-start | bytes 49156
  1.0 7.6 %collective-permute-start = (bf16[16,2,16,128]{3,2,1,0:T(8,128)(2,1)S(1)}, bf16[16,2,16,128]{3,2,1,0:T(8,128)(2,1)S(1)}, u32[]{:S(2)}, u32[]{:S(2)}) collective-permute-start(bf16[16,2,16,128]{3,2,1,0:T(8,128)(2,1)S(1)} %get-tuple-element.12), channel_id=1, source_target_pairs={{0,8},{8,16},{16,24},{1,9},{9,17},{17,25},{2,10},{10,18},{18,26},{... | collective-permute-start | bytes 393224 | tf_op jit(solution)/shard_map/ppermute | solution.py:218
  5.9 7.5 %collective-permute-start.1 = (bf16[16,2,16,128]{3,2,1,0:T(8,128)(2,1)S(1)}, bf16[16,2,16,128]{3,2,1,0:T(8,128)(2,1)S(1)}, u32[]{:S(2)}, u32[]{:S(2)}) collective-permute-start(bf16[16,2,16,128]{3,2,1,0:T(8,128)(2,1)S(1)} %get-tuple-element.11), channel_id=1, source_target_pairs={{8,0},{16,8},{24,16},{9,1},{17,9},{25,17},{10,2},{18,10},{26,18},{... | collective-permute-start | bytes 393224 | tf_op jit(solution)/shard_map/ppermute | solution.py:218
  8.0 11.8 %copy-start.14 = (bf16[27,16,16]{0,2,1:T(8,128)(2,1)S(1)}, bf16[27,16,16]{0,2,1:T(8,128)(2,1)}, u32[]{:S(2)}) copy-start(bf16[27,16,16]{0,2,1:T(8,128)(2,1)} %param.18) | copy-start | bytes 41476
  8.6 11.6 %copy-start.15 = (bf16[27,16,16]{0,2,1:T(8,128)(2,1)S(1)}, bf16[27,16,16]{0,2,1:T(8,128)(2,1)}, u32[]{:S(2)}) copy-start(bf16[27,16,16]{0,2,1:T(8,128)(2,1)} %param.19) | copy-start | bytes 41476
  13.4 6.5 %copy-start.11 = (bf16[16,36,16,128]{3,2,1,0:T(8,128)(2,1)}, bf16[16,36,16,128]{3,2,1,0:T(8,128)(2,1)S(1)}, u32[]{:S(2)}) copy-start(bf16[16,36,16,128]{3,2,1,0:T(8,128)(2,1)S(1)} %constant_dynamic-update-slice_fusion.own_ref) | copy-start | bytes 7077892
  13.9 10.8 %copy-start.17 = (u32[32]{0:T(128)S(1)}, u32[32]{0:T(128)}, u32[]{:S(2)}) copy-start(u32[32]{0:T(128)} %constant.67) | copy-start | bytes 388
  13.9 11.4 %copy-start.10 = (s32[864,1]{1,0:T(8,128)S(1)}, s32[864,1]{1,0:T(8,128)}, u32[]{:S(2)}) copy-start(s32[864,1]{1,0:T(8,128)} %constant.53.clone) | copy-start | bytes 10372
  13.9 11.4 %copy-start.12 = (pred[864,1]{1,0:T(32,128)(4,1)S(1)}, pred[864,1]{1,0:T(32,128)(4,1)}, u32[]{:S(2)}) copy-start(pred[864,1]{1,0:T(32,128)(4,1)} %constant.64) | copy-start | bytes 2596
  13.9 11.4 %copy-start.13 = (pred[864,1]{1,0:T(32,128)(4,1)S(1)}, pred[864,1]{1,0:T(32,128)(4,1)}, u32[]{:S(2)}) copy-start(pred[864,1]{1,0:T(32,128)(4,1)} %constant.63) | copy-start | bytes 2596
  14.7 10.7 %collective-permute-start.3 = (bf16[36,32,128]{2,1,0:T(8,128)(2,1)}, bf16[36,32,128]{2,1,0:T(8,128)(2,1)}, u32[]{:S(2)}, u32[]{:S(2)}) collective-permute-start(bf16[36,32,128]{2,1,0:T(8,128)(2,1)} %bitcast.3), channel_id=1, source_target_pairs={{1,0},{2,1},{3,2},{4,3},{5,4},{6,5},{7,6},{9,8},{10,9},{11,10},{12... | collective-permute-start | bytes 884744 | tf_op jit(solution)/shard_map/ppermute | solution.py:218
  16.0 9.4 %collective-permute-start.2 = (bf16[36,32,128]{2,1,0:T(8,128)(2,1)S(1)}, bf16[36,32,128]{2,1,0:T(8,128)(2,1)}, u32[]{:S(2)}, u32[]{:S(2)}) collective-permute-start(bf16[36,32,128]{2,1,0:T(8,128)(2,1)S(1)} %bitcast.110), channel_id=1, source_target_pairs={{0,1},{1,2},{2,3},{3,4},{4,5},{5,6},{6,7},{8,9},{9,10},{10,11},{11... | collective-permute-start | bytes 884744 | tf_op jit(solution)/shard_map/ppermute | solution.py:218
  20.6 6.0 %copy-start.1 = (s32[768,1]{1,0:T(8,128)S(1)}, s32[768,1]{1,0:T(8,128)}, u32[]{:S(2)}) copy-start(s32[768,1]{1,0:T(8,128)} %constant.57.clone.oy2) | copy-start | bytes 9220
  20.6 6.0 %copy-start.2 = (bf16[864,48]{1,0:T(8,128)(2,1)S(1)}, bf16[864,48]{1,0:T(8,128)(2,1)}, u32[]{:S(2)}) copy-start(bf16[864,48]{1,0:T(8,128)(2,1)} %constant.51.clone.l1) | copy-start | bytes 248836
  20.7 6.0 %copy-start.3 = (bf16[768,48]{1,0:T(8,128)(2,1)S(1)}, bf16[768,48]{1,0:T(8,128)(2,1)}, u32[]{:S(2)}) copy-start(bf16[768,48]{1,0:T(8,128)(2,1)} %constant.55.clone.l2) | copy-start | bytes 221188
  20.7 6.0 %copy-start.4 = (bf16[48,960]{1,0:T(8,128)(2,1)S(1)}, bf16[48,960]{1,0:T(8,128)(2,1)}, u32[]{:S(2)}) copy-start(bf16[48,960]{1,0:T(8,128)(2,1)} %constant.52.clone.r1) | copy-start | bytes 276484
  20.7 5.9 %copy-start.5 = (bf16[48,864]{1,0:T(8,128)(2,1)S(1)}, bf16[48,864]{1,0:T(8,128)(2,1)}, u32[]{:S(2)}) copy-start(bf16[48,864]{1,0:T(8,128)(2,1)} %constant.56.clone.r2) | copy-start | bytes 248836
  20.7 5.9 %copy-start.6 = (f32[128,8]{1,0:T(8,128)S(1)}, f32[128,8]{1,0:T(8,128)}, u32[]{:S(2)}) copy-start(f32[128,8]{1,0:T(8,128)} %constant.60.clone.lanes_ref) | copy-start | bytes 12292
  20.7 5.9 %copy-start.7 = (f32[16,256]{1,0:T(8,128)S(1)}, f32[16,256]{1,0:T(8,128)}, u32[]{:S(2)}) copy-start(f32[16,256]{1,0:T(8,128)} %constant.59.clone.cells_ref) | copy-start | bytes 49156
  20.7 5.9 %copy-start.8 = (s32[1,960]{1,0:T(1,128)S(1)}, s32[1,960]{1,0:T(1,128)}, u32[]{:S(2)}) copy-start(s32[1,960]{1,0:T(1,128)} %constant.54.clone.iy1) | copy-start | bytes 11524
  20.7 5.9 %copy-start.9 = (s32[1,864]{1,0:T(1,128)S(1)}, s32[1,864]{1,0:T(1,128)}, u32[]{:S(2)}) copy-start(s32[1,864]{1,0:T(1,128)} %constant.58.clone.iy2) | copy-start | bytes 10372
  111.7 34.6 %copy-start.16 = (bf16[16,32]{1,0:T(8,128)(2,1)S(1)}, bf16[16,32]{1,0:T(8,128)(2,1)}, u32[]{:S(2)}) copy-start(bf16[16,32]{1,0:T(8,128)(2,1)} %param.23) | copy-start | bytes 3076

commit v2 on v1

--- a/solution.py
+++ b/solution.py
@@ -8,6 +8,8 @@
 
 POOL = 16
 FAR = 4096
+LANES = 128
+MESH = pl.DeviceIdType.MESH
 VMEM_LIMIT = 48 * 1024 * 1024
 
 
@@ -67,6 +69,13 @@
     )
 
 
+def nt_dot(a, b, precision=None, transposed=True):
+    return lax.dot_general(
+        a, b, (((1,), (1 if transposed else 0,)), ((), ())),
+        precision=precision, preferred_element_type=jnp.float32,
+    )
+
+
 def fine_kernel(
     own_ref, rim_ref, w1_ref, w2_ref, l1, r1, oy1, iy1, l2, r2, oy2, iy2, edge_ref, cells_ref,
     lanes_ref, second_ref, pooled_ref, m1_ref, m2_ref, first_ref, sums_ref,
@@ -118,9 +127,8 @@
             cells_ref[...], sums_ref[block],
             precision=lax.Precision.HIGHEST, preferred_element_type=jnp.float32,
         )
-        pooled_ref[block] = jnp.dot(
-            by_row, lanes_ref[...],
-            precision=lax.Precision.HIGHEST, preferred_element_type=jnp.float32,
+        pooled_ref[block] = nt_dot(
+            lanes_ref[...], jnp.transpose(by_row), lax.Precision.HIGHEST, False
         ) / float(POOL**3)
 
 
@@ -139,8 +147,9 @@
 
     edge = jnp.stack([at_x > 0, at_x < along_x - 1]).astype(jnp.float32)
     edge = jnp.broadcast_to(edge[:, None], (2, depth))
-    cells = jnp.asarray(np.repeat(np.eye(chans, dtype=np.float32), size_y, axis=1))
-    lanes = jnp.asarray(np.repeat(np.eye(depth // POOL, dtype=np.float32), POOL, axis=0))
+    cells = np.repeat(np.eye(chans, dtype=np.float32), size_y, axis=1)
+    cells = jnp.asarray(np.pad(cells, ((0, LANES - chans), (0, 0))))
+    lanes = jnp.asarray(np.repeat(np.eye(depth // POOL, dtype=np.float32), POOL, axis=1))
     rows1, rows2 = l1.shape[0] // 3, l2.shape[0] // 3
     cols1, cols2 = r1.shape[1], r2.shape[1]
     spec = pl.BlockSpec(memory_space=pltpu.VMEM)
@@ -149,7 +158,7 @@
         fine_kernel,
         out_shape=(
             jax.ShapeDtypeStruct((size_x, rows2, depth), jnp.bfloat16),
-            jax.ShapeDtypeStruct((size_x // POOL, chans, depth // POOL), jnp.float32),
+            jax.ShapeDtypeStruct((size_x // POOL, depth // POOL, LANES), jnp.float32),
         ),
         in_specs=[spec] * 15,
         out_specs=(spec, spec),
@@ -186,7 +195,6 @@
     size_x, rows, depth = second.shape
     chans = w_skip.shape[0]
     size_y = rows // chans
-    up = jnp.repeat(jnp.repeat(up, POOL, axis=2), size_y, axis=1)
     matrix = w_skip[:, None, :, None] * jnp.eye(size_y, dtype=w_skip.dtype)[None, :, None, :]
     matrix = matrix.reshape(rows, rows)
     step = 8
@@ -208,67 +216,289 @@
     )(second, up, matrix)
 
 
+def halo_kernel(nx, ny, features_ref, side_ref, zero_ref, zero_side_ref, own_ref, rim_ref, send, recv, local):
+    at_x, at_y = lax.axis_index("gx"), lax.axis_index("gy")
+    size_x = features_ref.shape[1]
+    rows = side_ref.shape[2]
+
+    def exists(dx, dy):
+        x, y = at_x + dx, at_y + dy
+        return (x >= 0) & (x < nx) & (y >= 0) & (y < ny)
+
+    around = [(dx, dy) for dx in (-1, 0, 1) for dy in (-1, 0, 1) if (dx, dy) != (0, 0)]
+    barrier = pltpu.get_barrier_semaphore()
+    for dx, dy in around:
+
+        @pl.when(exists(dx, dy))
+        def _():
+            pl.semaphore_signal(
+                barrier, inc=1, device_id=(at_x + dx, at_y + dy), device_id_type=MESH
+            )
+
+    wide = 3 - (at_x == 0).astype(jnp.int32) - (at_x == nx - 1).astype(jnp.int32)
+    high = 3 - (at_y == 0).astype(jnp.int32) - (at_y == ny - 1).astype(jnp.int32)
+    pl.semaphore_wait(barrier, wide * high - 1)
+
+    taken = {-1: (0, 2), 0: (0, size_x), 1: (size_x - 2, 2)}
+    landed = {-1: (size_x + 2, 2), 0: (2, size_x), 1: (0, 2)}
+
+    def place(dx, dy):
+        start, count = landed[dx]
+        if dy == 0:
+            return own_ref.at[:, start : start + count]
+        row = 0 if dy == 1 else rows
+        return rim_ref.at[start : start + count, row : row + rows]
+
+    def sent(index, dx, dy):
+        start, count = taken[dx]
+        if dy == 0:
+            source = features_ref.at[:, start : start + count]
+        else:
+            source = side_ref.at[0 if dy == 1 else 1, start : start + count]
+        return pltpu.make_async_remote_copy(
+            src_ref=source, dst_ref=place(dx, dy), send_sem=send.at[index],
+            recv_sem=recv.at[index],
+            device_id=(lax.rem(at_x + dx + nx, nx), lax.rem(at_y + dy + ny, ny)),
+            device_id_type=MESH,
+        )
+
+    def blank(index, dx, dy):
+        count = landed[dx][1]
+        source = zero_ref if dy == 0 else zero_side_ref.at[0:count]
+        return pltpu.make_async_copy(source, place(dx, dy), local.at[index])
+
+    for index, (dx, dy) in enumerate(around):
+
+        @pl.when(exists(dx, dy))
+        def _():
+            sent(index, dx, dy).start()
+
+        @pl.when(jnp.logical_not(exists(-dx, -dy)))
+        def _():
+            blank(index, dx, dy).start()
+
+    middle = pltpu.make_async_copy(
+        features_ref, own_ref.at[:, 2 : size_x + 2], local.at[len(around)]
+    )
+    middle.start()
+    for index, (dx, dy) in enumerate(around):
+
+        @pl.when(exists(-dx, -dy))
+        def _():
+            sent(index, dx, dy).wait_recv()
+
+        @pl.when(jnp.logical_not(exists(-dx, -dy)))
+        def _():
+            blank(index, dx, dy).wait()
+
+        @pl.when(exists(dx, dy))
+        def _():
+            sent(index, dx, dy).wait_send()
+
+    middle.wait()
+
+
 def halo(features):
     chans, size_x, size_y, depth = features.shape
     nx, ny = lax.axis_size("gx"), lax.axis_size("gy")
 
-    def both(axis, count, last, leading):
-        up = [(i, i + 1) for i in range(count - 1)]
-        down = [(j, i) for i, j in up]
-        return lax.ppermute(last, axis, up), lax.ppermute(leading, axis, down)
-
-    before, after = both("gx", nx, features[:, size_x - 2 :], features[:, :2])
-    own = jnp.concatenate([before, features, after], axis=1)
-
     def side(v):
-        return jnp.transpose(v, (1, 2, 0, 3)).reshape(size_x + 4, 2 * chans, depth)
-
-    below, above = both("gy", ny, side(own[:, :, size_y - 2 :]), side(own[:, :, :2]))
-    return own, jnp.concatenate([below, above], axis=1)
-
-
-def coarse_level(pooled, w_lift, w_coarse, w_decode):
-    block_x, chans, block_z = pooled.shape
-    nx, ny = lax.axis_size("gx"), lax.axis_size("gy")
+        return jnp.transpose(v, (1, 2, 0, 3)).reshape(size_x, 2 * chans, depth)
+
+    sides = jnp.stack([side(features[:, :, size_y - 2 :]), side(features[:, :, :2])])
+    anywhere = pl.BlockSpec(memory_space=pl.ANY)
+    return pl.pallas_call(
+        lambda *refs: halo_kernel(nx, ny, *refs),
+        out_shape=(
+            jax.ShapeDtypeStruct((chans, size_x + 4, size_y, depth), jnp.bfloat16),
+            jax.ShapeDtypeStruct((size_x + 4, 4 * chans, depth), jnp.bfloat16),
+        ),
+        in_specs=[anywhere] * 4,
+        out_specs=(anywhere, anywhere),
+        scratch_shapes=[
+            pltpu.SemaphoreType.DMA((8,)),
+            pltpu.SemaphoreType.DMA((8,)),
+            pltpu.SemaphoreType.DMA((9,)),
+        ],
+        compiler_params=pltpu.CompilerParams(collective_id=0, has_side_effects=True),
+        name="halo",
+    )(
+        features, sides, jnp.zeros((chans, 2, size_y, depth), jnp.bfloat16),
+        jnp.zeros((size_x, 2 * chans, depth), jnp.bfloat16),
+    )
+
+
+def coarse_kernel(
+    nx, ny, pooled_ref, lift_ref, weight_ref, decode_ref, join_ref, cells_ref, lanes_ref, up_ref,
+    near_ref, field_ref, lifted_ref, part_ref, parts_ref,
+    send_x, recv_x, send_y, recv_y, send_p, recv_p,
+):
     at_x, at_y = lax.axis_index("gx"), lax.axis_index("gy")
-    every = lax.all_gather(pooled, ("gx", "gy"), axis=0)
-    every = every.reshape(nx, ny, block_x, chans, block_z)
-    every = jnp.transpose(every, (0, 2, 1, 4, 3)).reshape(nx * block_x, ny, block_z, chans)
-    every = jnp.pad(every, ((1, 1), (1, 1), (1, 1), (0, 0)))
-    near = lax.dynamic_slice_in_dim(every, at_x * block_x, block_x + 2, axis=0)
-    raised = jnp.einsum(
-        "xyzc,oc->xyzo", near, w_lift.astype(jnp.float32), precision=lax.Precision.HIGHEST
-    )
-    lifted = jnp.maximum(raised, 0.0).astype(jnp.bfloat16)
-    windows = []
+    block_x, block_z, lanes = pooled_ref.shape
+    peers = [lax.rem(at_y + step, ny) for step in range(1, ny)]
+    has_low, has_high = at_x > 0, at_x < nx - 1
+
+    barrier = pltpu.get_barrier_semaphore()
+    for peer in peers:
+        pl.semaphore_signal(barrier, inc=1, device_id=(at_x, peer), device_id_type=MESH)
+
+    @pl.when(has_low)
+    def _():
+        pl.semaphore_signal(barrier, inc=1, device_id=(at_x - 1, at_y), device_id_type=MESH)
+
+    @pl.when(has_high)
+    def _():
+        pl.semaphore_signal(barrier, inc=1, device_id=(at_x + 1, at_y), device_id_type=MESH)
+
+    pl.semaphore_wait(
+        barrier, ny - 1 + has_low.astype(jnp.int32) + has_high.astype(jnp.int32)
+    )
+
+    def beside(index):
+        source, place, target = (
+            (block_x - 1, 0, lax.rem(at_x + 1, nx)),
+            (0, block_x + 1, lax.rem(at_x + nx - 1, nx)),
+        )[index]
+        return pltpu.make_async_remote_copy(
+            src_ref=pooled_ref.at[source], dst_ref=near_ref.at[place],
+            send_sem=send_x.at[index], recv_sem=recv_x.at[index],
+            device_id=(target, at_y), device_id_type=MESH,
+        )
+
+    blank = jnp.zeros((block_z, lanes), jnp.float32)
+
+    @pl.when(has_high)
+    def _():
+        beside(0).start()
+
+    @pl.when(has_low)
+    def _():
+        beside(1).start()
+
+    near_ref[1 : block_x + 1] = pooled_ref[...]
+    field_ref[0] = jnp.zeros(field_ref.shape[1:], jnp.float32)
+    field_ref[ny + 1] = jnp.zeros(field_ref.shape[1:], jnp.float32)
+    lifted_ref[...] = jnp.zeros_like(lifted_ref)
+
+    @pl.when(has_low)
+    def _():
+        beside(0).wait_recv()
+
+    @pl.when(has_high)
+    def _():
+        beside(1).wait_recv()
+
+    @pl.when(jnp.logical_not(has_low))
+    def _():
+        near_ref[0] = blank
+
+    @pl.when(jnp.logical_not(has_high))
+    def _():
+        near_ref[block_x + 1] = blank
+
+    gather = []
+    for step, peer in enumerate(peers):
+        copy = pltpu.make_async_remote_copy(
+            src_ref=near_ref, dst_ref=field_ref.at[at_y + 1],
+            send_sem=send_y.at[step], recv_sem=recv_y.at[step],
+            device_id=(at_x, peer), device_id_type=MESH,
+        )
+        copy.start()
+        gather.append(copy)
+    field_ref[at_y + 1] = near_ref[...]
+    for copy in gather:
+        copy.wait_recv()
+
+    field = field_ref[...].reshape((ny + 2) * (block_x + 2) * block_z, lanes)
+    raised = nt_dot(field, lift_ref[...], lax.Precision.HIGHEST, False)
+    raised = jnp.maximum(raised, 0.0).astype(jnp.bfloat16).astype(jnp.float32)
+    wide = raised.shape[1]
+    lifted_ref[:, :, block_z : 2 * block_z] = raised.reshape(ny + 2, block_x + 2, block_z, wide)
+    count = ny * block_x * block_z
+    total = jnp.zeros((count, weight_ref.shape[1]), jnp.float32)
     for offset in range(27):
         a, b, c = offset // 9, offset // 3 % 3, offset % 3
-        cut = lifted[a : a + block_x, b : b + ny, c : c + block_z]
-        windows.append(cut.reshape(block_x * ny * block_z, -1))
-    stacked = jnp.concatenate(windows, axis=1)
-    count = w_coarse.shape[0]
-    total = lax.dot_general(
-        stacked, w_coarse.reshape(count, -1), (((1,), (1,)), ((), ())),
-        preferred_element_type=jnp.float32,
-    )
+        low = block_z - 1 + c
+        cut = lifted_ref[b : b + ny, a : a + block_x, low : low + block_z]
+        cut = cut.reshape(count, wide).astype(jnp.bfloat16)
+        total = total + nt_dot(cut, weight_ref[offset])
     coarse = jnp.maximum(total, 0.0).astype(jnp.bfloat16)
-    mine = lax.dynamic_slice_in_dim(w_decode, at_y * count, count, axis=1)
-    part = lax.dot_general(
-        coarse, mine, (((1,), (1,)), ((), ())), preferred_element_type=jnp.float32
-    )
-    part = jnp.transpose(part.reshape(block_x, ny, block_z, chans), (1, 0, 3, 2))
-    whole = lax.psum_scatter(part, "gy", scatter_dimension=0, tiled=False)
-    return whole.astype(jnp.bfloat16)
+    part = jnp.dot(coarse, decode_ref[...], preferred_element_type=jnp.float32)
+    part_ref[...] = part.reshape(part_ref.shape)
+    scatter = []
+    for step, peer in enumerate(peers):
+        copy = pltpu.make_async_remote_copy(
+            src_ref=part_ref.at[peer], dst_ref=parts_ref.at[at_y],
+            send_sem=send_p.at[step], recv_sem=recv_p.at[step],
+            device_id=(at_x, peer), device_id_type=MESH,
+        )
+        copy.start()
+        scatter.append(copy)
+    parts_ref[at_y] = part_ref[at_y]
+    for copy in scatter:
+        copy.wait_recv()
+    decoded = jnp.sum(parts_ref[...], axis=0).astype(jnp.bfloat16)
+    up = jnp.dot(decoded, join_ref[...], preferred_element_type=jnp.float32)
+    for block in range(block_x):
+        mine = up[block * block_z : (block + 1) * block_z]
+        mine = nt_dot(jnp.transpose(mine), lanes_ref[...], lax.Precision.HIGHEST, False)
+        up_ref[block] = nt_dot(cells_ref[...], mine, lax.Precision.HIGHEST, False)
+
+    @pl.when(has_high)
+    def _():
+        beside(0).wait_send()
+
+    @pl.when(has_low)
+    def _():
+        beside(1).wait_send()
+
+    for copy in gather + scatter:
+        copy.wait_send()
+
+
+def coarse_level(pooled, w_lift, w_coarse, w_decode, w_up, size_y):
+    block_x, block_z, lanes = pooled.shape
+    nx, ny = lax.axis_size("gx"), lax.axis_size("gy")
+    count, _, wide = w_coarse.shape
+    chans = w_up.shape[0]
+    more = lanes - chans
+    lift = jnp.pad(w_lift.astype(jnp.float32).T, ((0, more), (0, 0)))
+    mine = lax.dynamic_slice_in_dim(w_decode, lax.axis_index("gy") * count, count, axis=1)
+    decode = jnp.pad(mine.T, ((0, 0), (0, more)))
+    joining = jnp.pad(w_up.T, ((0, more), (0, more)))
+    cells = np.repeat(np.eye(chans, dtype=np.float32), size_y, axis=0)
+    cells = jnp.asarray(np.pad(cells, ((0, 0), (0, more))))
+    spread = jnp.asarray(np.repeat(np.eye(block_z, dtype=np.float32), POOL, axis=1))
+    spec = pl.BlockSpec(memory_space=pltpu.VMEM)
+    vector = lambda *shape: pltpu.VMEM(shape, jnp.float32)
+    return pl.pallas_call(
+        lambda *refs: coarse_kernel(nx, ny, *refs),
+        out_shape=jax.ShapeDtypeStruct((block_x, chans * size_y, block_z * POOL), jnp.float32),
+        in_specs=[spec] * 7,
+        out_specs=spec,
+        scratch_shapes=[
+            vector(block_x + 2, block_z, lanes),
+            vector(ny + 2, block_x + 2, block_z, lanes),
+            vector(ny + 2, block_x + 2, 3 * block_z, wide),
+            vector(ny, block_x * block_z, lanes),
+            vector(ny, block_x * block_z, lanes),
+            pltpu.SemaphoreType.DMA((2,)),
+            pltpu.SemaphoreType.DMA((2,)),
+        ] + [pltpu.SemaphoreType.DMA((ny - 1,))] * 4,
+        compiler_params=pltpu.CompilerParams(
+            collective_id=1, has_side_effects=True, vmem_limit_bytes=VMEM_LIMIT
+        ),
+        name="coarse",
+    )(
+        pooled, lift, jnp.transpose(w_coarse, (1, 0, 2)), decode, joining, cells, spread,
+    )
 
 
 def local(features, w_first, w_second, w_lift, w_coarse, w_decode, w_joining):
     chans, size_x, size_y, depth = features.shape
     own, rim = halo(features)
     second, pooled = fine(own, rim, w_first, w_second, size_x)
-    decoded = coarse_level(pooled, w_lift, w_coarse, w_decode)
-    up = jnp.einsum(
-        "oc,xcz->xoz", w_joining[:, chans:], decoded, preferred_element_type=jnp.float32
-    )
+    up = coarse_level(pooled, w_lift, w_coarse, w_decode, w_joining[:, chans:], size_y)
     return join(second, up, w_joining[:, :chans])
 
 

time: 150 us -> 144 us (0.960)
  Pallas kernels: 30.7 us -> 129 us
  blocking collectives: 68 us -> 0 us
  local copies, waits for them, and re-layouts: 29.1 us -> 11.6 us
  starting transfers between devices: 11.2 us -> 0 us
  matrix products: 5.45 us -> 0 us
  waiting for transfers between devices: 3.08 us -> 0 us
    pallas_call x0 -> x2, Pallas kernels: none -> 97.7 us  [the longest x1 81.2 us: halo(): pl.pallas_call(lambda *refs: halo_kernel(nx, ny, *refs), out_shape=(jax.S...]
    all_gather x1 -> x0, blocking collectives: 41.4 us -> none  [coarse_level(): every = lax.all_gather(pooled, ('gx', 'gy'), axis=0)]
    unnamed x1 -> x0, blocking collectives: 26.6 us -> none
    unnamed x67 -> x38, local copies, waits for them, and re-layouts: 21 us -> 5.86 us
    ppermute x4 -> x0, starting transfers between devices: 11.2 us -> none  [both(): return (lax.ppermute(last, axis, up), lax.ppermute(leading, axis, down))]
    dot_general x3 -> x0, matrix products: 5.45 us -> none  [the longest x1 4.01 us: coarse_level(): lax.dot_general(coarse, mine, (((1,), (1,)), ((), ())), preferred_element...]
    ppermute x4 -> x0, waiting for transfers between devices: 3.08 us -> none  [both(): return (lax.ppermute(last, axis, up), lax.ppermute(leading, axis, down))]
    reshape x3 -> x0, local copies, waits for them, and re-layouts: 3.03 us -> none  [the longest x1 2.91 us: coarse_level(): w_coarse.reshape(count, -1)]
  transfers between devices with their start and end apart: 4 -> 0, of which waited for: 2 -> 0; matrix products, arithmetic and copies ran while one was open for 6% -> 0% of each run, Pallas kernels for 0% -> 0%
where the time goes in v2:
time: 144 us; the launch traced here: 143 us
  Pallas kernels  129 us (90%)
  local copies, waits for them, and re-layouts  11.6 us (8%)
  other arithmetic  2.28 us (2%)
    pallas_call x1, Pallas kernels, halo(): pl.pallas_call(lambda *refs: halo_kernel(nx, ny, *refs), out_shape=(jax.S...  81.2 us
    pallas_call x1, Pallas kernels, fine(): pl.pallas_call(fine_kernel, out_shape=(jax.ShapeDtypeStruct((size_x, rows...  28.4 us
    pallas_call x1, Pallas kernels, coarse_level(): pl.pallas_call(lambda *refs: coarse_kernel(nx, ny, *refs), out_shape=jax....  16.5 us
    unnamed x38, local copies, waits for them, and re-layouts  5.86 us

profile of v2, /device:TPU:0, one launch (start us, length us, event | category | flops | bytes accessed | tf_op | source)
XLA Modules:
  0.0 142.8 jit_solution(8514984376673505633)
XLA Ops:
  0.0 0.0 copy-start
  0.0 1.2 or_select_fusion.oy1
  1.2 0.1 add_convert_fusion
  1.3 0.1 broadcast_in_dim.21.edge_ref
  1.4 2.1 %slice_bitcast_fusion.1 = (bf16[32,2,16,128]{3,1,0,2:T(2,128)(2,1)S(1)}, bf16[32,2,16,128]{3,1,0,2:T(2,128)(2,1)S(1)}) fusion(bf16[16,32,16,128]{3,2,1,0:T(8,128)(2,1)} %refs_0_.1), kind=kLoop, calls=%fused_computation.4 | loop fusion | bytes 1048576 | tf_op jit(solution)/shard_map/transpose | solution.py:306
  3.5 0.3 copy.26
  3.8 0.3 copy.27
  4.1 0.0 copy-start.13
  4.1 0.8 pad_maximum_fusion.refs_1_
  5.0 0.0 copy-start.14
  5.0 0.7 broadcast_in_dim.19.refs_3_
  5.7 0.7 broadcast_in_dim.18.refs_2_
  6.4 0.0 copy-start.3
  6.4 0.0 copy-start.5
  6.4 0.0 copy-start.6
  6.4 0.0 copy-start.8
  6.4 0.0 copy-start.11
  6.4 0.0 copy-start.12
  6.4 81.2 %halo.1 = (bf16[16,36,16,128]{3,2,1,0:T(8,128)(2,1)}, bf16[36,64,128]{2,1,0:T(8,128)(2,1)}) custom-call(bf16[16,32,16,128]{3,2,1,0:T(8,128)(2,1)} %refs_0_.1, bf16[2,32,32,128]{3,2,1,0:T(8,128)(2,1)} %pad_maximum_fusion.refs_1_, bf16[16,2,16,128]{3,2,1,0:T(8,128)(2,1)} %broadcast_in_dim.18.refs_2_, bf16[32,32,128]{2,1,0:T(8,128)(2,1)} %broadcast_in_dim.19.refs_3_), custom_call_target="tpu_custom_call" | custom-call | tf_op jit(solution)/shard_map/halo/pallas_call | solution.py:310
  87.7 0.0 copy-done.13
  87.7 0.2 copy.28
  87.9 0.1 copy.29
  87.9 0.1 reshape.43.w1_ref
  88.1 0.0 copy-done.14
  88.1 0.2 copy.30
  88.3 0.1 copy.31
  88.3 0.1 reshape.45.w2_ref
  88.5 0.0 copy-done.3
  88.5 0.0 copy-done.5
  88.5 0.0 copy-done.6
  88.5 0.0 copy-done.8
  88.5 0.0 copy-done.11
  88.5 0.0 copy-done.12
  88.5 0.0 copy-start.4
  88.5 1.1 copy-done.4
  89.6 0.0 copy-start.7
  89.6 0.9 copy-done.7
  90.5 0.0 copy-start.9
  90.5 0.9 copy-done.9
  91.4 0.0 copy-start.10
  91.4 0.9 copy-done.10
  92.3 0.0 copy-start.16
  92.3 0.0 copy-start.15
  92.3 0.0 copy-start.2
  92.3 28.4 %fine.1 = (bf16[32,256,128]{2,1,0:T(8,128)(2,1)S(1)}, f32[2,8,128]{2,1,0:T(8,128)S(1)}) custom-call(bf16[16,36,16,128]{3,2,1,0:T(8,128)(2,1)} %get-tuple-element.9.own_ref, bf16[36,64,128]{2,1,0:T(8,128)(2,1)S(1)} %copy-done.4, bf16[3,48,48]{2,1,0:T(8,128)(2,1)S(1)} %reshape.43.w1_ref, bf16[3,48,48]{2,1,0:T(8,128)(2,1)S(1)} %reshape.45.w2_ref, ...), custom_call_target="tpu_custom_call" | custom-call | flops 12655263744 | bytes 8000000 | tf_op jit(solution)/shard_map/fine/pallas_call | solution.py:157
  120.7 0.0 copy-done
  120.7 0.1 constant_dynamic-slice_fusion
  120.8 0.1 copy.34
  121.0 0.0 copy-done.16
  121.0 0.1 fusion.1
  121.0 0.1 copy.35
  121.1 0.0 copy-done.15
  121.2 0.0 copy-done.2
  121.2 0.0 copy-start.1
  121.2 1.5 %copy-done.1 = bf16[64,27,512]{2,0,1:T(8,128)(2,1)S(1)} copy-done((bf16[64,27,512]{2,0,1:T(8,128)(2,1)S(1)}, bf16[64,27,512]{2,0,1:T(8,128)(2,1)}, u32[]{:S(2)}) %copy-start.1) | copy-done | bytes 1769496
  122.7 16.5 %coarse.1.up_ref = f32[2,256,128]{2,1,0:T(8,128)S(1)} custom-call(f32[2,8,128]{2,1,0:T(8,128)S(1)} %get-tuple-element.12.refs_0_, f32[128,512]{1,0:T(8,128)S(1)} %pad_convert_fusion.refs_1_, bf16[27,64,512]{2,1,0:T(8,128)(2,1)S(1)} %bitcast.20, bf16[64,128]{1,0:T(8,128)(2,1)S(1)} %pad.16.refs_3_, bf16[128,128]{1,0:T(8,128)(2,1)S(1)} %pad.17.refs_4_, ...), custom_call_target="tpu_custom_call" | custom-call | tf_op jit(solution)/shard_map/coarse/pallas_call | solution.py:474
  139.1 0.1 broadcast_multiply_fusion
  139.3 1.0 mul.24.matrix_ref
  140.3 2.6 %join.1 = bf16[16,32,16,128]{3,2,1,0:T(8,128)(2,1)} custom-call(bf16[32,256,128]{2,1,0:T(8,128)(2,1)S(1)} %get-tuple-element.11.second_ref, f32[2,256,128]{2,1,0:T(8,128)S(1)} %coarse.1.up_ref, bf16[256,256]{1,0:T(8,128)(2,1)S(1)} %mul.24.matrix_ref), custom_call_target="tpu_custom_call" | custom-call | flops 536870912 | bytes 5000000 | tf_op jit(solution)/shard_map/join/pallas_call | solution.py:201
  (4 shorter events, 0.0 us)
Async XLA Ops:
  0.0 120.7 %copy-start = (bf16[16,512]{1,0:T(8,128)(2,1)S(1)}, bf16[16,512]{1,0:T(8,128)(2,1)}, u32[]{:S(2)}) copy-start(bf16[16,512]{1,0:T(8,128)(2,1)} %param.24) | copy-start | bytes 49156
  4.1 83.6 %copy-start.13 = (bf16[27,16,16]{0,2,1:T(8,128)(2,1)S(1)}, bf16[27,16,16]{0,2,1:T(8,128)(2,1)}, u32[]{:S(2)}) copy-start(bf16[27,16,16]{0,2,1:T(8,128)(2,1)} %param.20) | copy-start | bytes 41476
  5.0 83.1 %copy-start.14 = (bf16[27,16,16]{0,2,1:T(8,128)(2,1)S(1)}, bf16[27,16,16]{0,2,1:T(8,128)(2,1)}, u32[]{:S(2)}) copy-start(bf16[27,16,16]{0,2,1:T(8,128)(2,1)} %param.21) | copy-start | bytes 41476
  6.4 82.1 %copy-start.3 = (f32[8,128]{1,0:T(8,128)S(1)}, f32[8,128]{1,0:T(8,128)}, u32[]{:S(2)}) copy-start(f32[8,128]{1,0:T(8,128)} %constant.60.clone.lanes_ref.refs_6_) | copy-start | bytes 12292
  6.4 82.1 %copy-start.5 = (s32[768,1]{1,0:T(8,128)S(1)}, s32[768,1]{1,0:T(8,128)}, u32[]{:S(2)}) copy-start(s32[768,1]{1,0:T(8,128)} %constant.57.clone.oy2) | copy-start | bytes 9220
  6.4 82.1 %copy-start.6 = (bf16[864,48]{1,0:T(8,128)(2,1)S(1)}, bf16[864,48]{1,0:T(8,128)(2,1)}, u32[]{:S(2)}) copy-start(bf16[864,48]{1,0:T(8,128)(2,1)} %constant.51.clone.l1) | copy-start | bytes 248836
  6.4 82.1 %copy-start.8 = (f32[128,256]{1,0:T(8,128)S(1)}, f32[128,256]{1,0:T(8,128)}, u32[]{:S(2)}) copy-start(f32[128,256]{1,0:T(8,128)} %constant.59.clone.cells_ref) | copy-start | bytes 393220
  6.4 82.1 %copy-start.11 = (s32[1,960]{1,0:T(1,128)S(1)}, s32[1,960]{1,0:T(1,128)}, u32[]{:S(2)}) copy-start(s32[1,960]{1,0:T(1,128)} %constant.54.clone.iy1) | copy-start | bytes 11524
  6.4 82.1 %copy-start.12 = (s32[1,864]{1,0:T(1,128)S(1)}, s32[1,864]{1,0:T(1,128)}, u32[]{:S(2)}) copy-start(s32[1,864]{1,0:T(1,128)} %constant.58.clone.iy2) | copy-start | bytes 10372
  88.5 1.1 copy-start.4
  89.6 0.9 copy-start.7
  90.5 0.9 copy-start.9
  91.4 0.9 copy-start.10
  92.3 28.6 %copy-start.16 = (bf16[16,32]{1,0:T(8,128)(2,1)S(1)}, bf16[16,32]{1,0:T(8,128)(2,1)}, u32[]{:S(2)}) copy-start(bf16[16,32]{1,0:T(8,128)(2,1)} %param.25) | copy-start | bytes 3076
  92.3 28.8 %copy-start.15 = (bf16[512,16]{0,1:T(8,128)(2,1)S(1)}, bf16[512,16]{0,1:T(8,128)(2,1)}, u32[]{:S(2)}) copy-start(bf16[512,16]{0,1:T(8,128)(2,1)} %param.22) | copy-start | bytes 49156
  92.3 28.9 %copy-start.2 = (f32[256,128]{1,0:T(8,128)S(1)}, f32[256,128]{1,0:T(8,128)}, u32[]{:S(2)}) copy-start(f32[256,128]{1,0:T(8,128)} %constant.61.clone.refs_5_) | copy-start | bytes 393220
  121.2 1.5 %copy-start.1 = (bf16[64,27,512]{2,0,1:T(8,128)(2,1)S(1)}, bf16[64,27,512]{2,0,1:T(8,128)(2,1)}, u32[]{:S(2)}) copy-start(bf16[64,27,512]{2,0,1:T(8,128)(2,1)} %param.23) | copy-start | bytes 5308420

commit v3 on v2

--- a/solution.py
+++ b/solution.py
@@ -76,20 +76,33 @@
     )
 
 
+def in_pairs(body, steps, group):
+    def pair(step, carry):
+        body(step * 2 * group)
+        body(step * 2 * group + group)
+        return carry
+
+    lax.fori_loop(0, steps // 2, pair, 0)
+    if steps % 2:
+        body((steps - 1) * group)
+
+
 def fine_kernel(
-    own_ref, rim_ref, w1_ref, w2_ref, l1, r1, oy1, iy1, l2, r2, oy2, iy2, edge_ref, cells_ref,
+    features_ref, beyond_ref, rim_ref, w1_ref, w2_ref, l1, r1, oy1, iy1, l2, r2, oy2, iy2, edge_ref, cells_ref,
     lanes_ref, second_ref, pooled_ref, m1_ref, m2_ref, first_ref, sums_ref,
+    own_ref,
 ):
-    chans, planes_in, size_y, depth = own_ref.shape
-    size_x = second_ref.shape[0]
+    chans, size_x, size_y, depth = features_ref.shape
+    own_ref[:, 0:2] = beyond_ref[0]
+    own_ref[:, 2 : size_x + 2] = features_ref[...]
+    own_ref[:, size_x + 2 :] = beyond_ref[1]
     group = 2
     build_matrix(w1_ref, l1, r1, oy1, iy1, m1_ref)
     build_matrix(w2_ref, l2, r2, oy2, iy2, m2_ref)
     rows1 = first_ref.shape[1]
     rows2 = second_ref.shape[1]
 
-    def one(step, carry):
-        at = step * group
+    def one(at):
         planes = []
         for k in range(group + 2):
             own = own_ref[:, at + k].reshape(chans * size_y, depth)
@@ -99,15 +112,13 @@
         sums = shift_sum(parts, rows1, group, depth)
         for k in range(group):
             first_ref[at + k] = jnp.maximum(sums[k], 0.0).astype(jnp.bfloat16)
-        return carry
-
-    lax.fori_loop(0, (size_x + 2) // group, one, 0)
+
+    in_pairs(one, (size_x + 2) // group, group)
     first_ref[0] = first_ref[0] * edge_ref[0:1, :].astype(jnp.bfloat16)
     first_ref[size_x + 1] = first_ref[size_x + 1] * edge_ref[1:2, :].astype(jnp.bfloat16)
     sums_ref[...] = jnp.zeros_like(sums_ref)
 
-    def two(step, carry):
-        at = step * group
+    def two(at):
         data = stack_planes([first_ref[at + k] for k in range(group + 2)], group)
         parts = jnp.dot(m2_ref[...], data, preferred_element_type=jnp.float32)
         sums = shift_sum(parts, rows2, group, depth)
@@ -119,9 +130,8 @@
             total = value if total is None else total + value
         block = at // POOL
         sums_ref[block] = sums_ref[block] + total
-        return carry
-
-    lax.fori_loop(0, size_x // group, two, 0)
+
+    in_pairs(two, size_x // group, group)
     for block in range(size_x // POOL):
         by_row = jnp.dot(
             cells_ref[...], sums_ref[block],
@@ -132,14 +142,14 @@
         ) / float(POOL**3)
 
 
-def fine(own, rim, w_first, w_second, size_x):
-    chans, _, size_y, depth = own.shape
+def fine(features, beyond, rim, w_first, w_second):
+    chans, size_x, size_y, depth = features.shape
     along_x, along_y = lax.axis_size("gx"), lax.axis_size("gy")
     at_x, at_y = lax.axis_index("gx"), lax.axis_index("gy")
     l1, r1, oy1, iy1 = spread_maps(chans, size_y, 1, 2)
     l2, r2, oy2, iy2 = spread_maps(chans, size_y, 0, 1)
-    beyond = ((at_y == 0) & (oy1 < 0)) | ((at_y == along_y - 1) & (oy1 >= size_y))
-    oy1 = jnp.where(beyond, FAR, oy1)
+    outside = ((at_y == 0) & (oy1 < 0)) | ((at_y == along_y - 1) & (oy1 >= size_y))
+    oy1 = jnp.where(outside, FAR, oy1)
 
     def by_offset(weight):
         taps = weight.reshape(3, 3, 3, chans, chans)
@@ -160,19 +170,20 @@
             jax.ShapeDtypeStruct((size_x, rows2, depth), jnp.bfloat16),
             jax.ShapeDtypeStruct((size_x // POOL, depth // POOL, LANES), jnp.float32),
         ),
-        in_specs=[spec] * 15,
+        in_specs=[spec] * 16,
         out_specs=(spec, spec),
         scratch_shapes=[
             pltpu.VMEM((3 * rows1, cols1), jnp.bfloat16),
             pltpu.VMEM((3 * rows2, cols2), jnp.bfloat16),
             pltpu.VMEM((size_x + 2, rows1, depth), jnp.bfloat16),
             pltpu.VMEM((size_x // POOL, rows2, depth), jnp.float32),
+            pltpu.VMEM((chans, size_x + 4, size_y, depth), jnp.bfloat16),
         ],
         compiler_params=pltpu.CompilerParams(vmem_limit_bytes=VMEM_LIMIT),
         cost_estimate=pl.CostEstimate(flops=flops, bytes_accessed=8_000_000, transcendentals=0),
         name="fine",
     )(
-        own, rim, by_offset(w_first), by_offset(w_second),
+        features, beyond, rim, by_offset(w_first), by_offset(w_second),
         l1, r1, oy1, iy1, l2, r2, oy2, iy2, edge, cells, lanes,
     )
 
@@ -216,7 +227,7 @@
     )(second, up, matrix)
 
 
-def halo_kernel(nx, ny, features_ref, side_ref, zero_ref, zero_side_ref, own_ref, rim_ref, send, recv, local):
+def halo_kernel(nx, ny, features_ref, side_ref, beyond_out, rim_out, beyond_ref, rim_ref, send, recv):
     at_x, at_y = lax.axis_index("gx"), lax.axis_index("gy")
     size_x = features_ref.shape[1]
     rows = side_ref.shape[2]
@@ -245,7 +256,7 @@
     def place(dx, dy):
         start, count = landed[dx]
         if dy == 0:
-            return own_ref.at[:, start : start + count]
+            return beyond_ref.at[0 if dx == 1 else 1]
         row = 0 if dy == 1 else rows
         return rim_ref.at[start : start + count, row : row + rows]
 
@@ -262,11 +273,6 @@
             device_id_type=MESH,
         )
 
-    def blank(index, dx, dy):
-        count = landed[dx][1]
-        source = zero_ref if dy == 0 else zero_side_ref.at[0:count]
-        return pltpu.make_async_copy(source, place(dx, dy), local.at[index])
-
     for index, (dx, dy) in enumerate(around):
 
         @pl.when(exists(dx, dy))
@@ -275,27 +281,21 @@
 
         @pl.when(jnp.logical_not(exists(-dx, -dy)))
         def _():
-            blank(index, dx, dy).start()
-
-    middle = pltpu.make_async_copy(
-        features_ref, own_ref.at[:, 2 : size_x + 2], local.at[len(around)]
-    )
-    middle.start()
+            spot = place(dx, dy)
+            spot[...] = jnp.zeros(spot.shape, spot.dtype)
+
     for index, (dx, dy) in enumerate(around):
 
         @pl.when(exists(-dx, -dy))
         def _():
             sent(index, dx, dy).wait_recv()
 
-        @pl.when(jnp.logical_not(exists(-dx, -dy)))
-        def _():
-            blank(index, dx, dy).wait()
-
         @pl.when(exists(dx, dy))
         def _():
             sent(index, dx, dy).wait_send()
 
-    middle.wait()
+    beyond_out[...] = beyond_ref[...]
+    rim_out[...] = rim_ref[...]
 
 
 def halo(features):
@@ -307,25 +307,24 @@
 
     sides = jnp.stack([side(features[:, :, size_y - 2 :]), side(features[:, :, :2])])
     anywhere = pl.BlockSpec(memory_space=pl.ANY)
+    within = pl.BlockSpec(memory_space=pltpu.VMEM)
     return pl.pallas_call(
         lambda *refs: halo_kernel(nx, ny, *refs),
         out_shape=(
-            jax.ShapeDtypeStruct((chans, size_x + 4, size_y, depth), jnp.bfloat16),
+            jax.ShapeDtypeStruct((2, chans, 2, size_y, depth), jnp.bfloat16),
             jax.ShapeDtypeStruct((size_x + 4, 4 * chans, depth), jnp.bfloat16),
         ),
-        in_specs=[anywhere] * 4,
-        out_specs=(anywhere, anywhere),
+        in_specs=[anywhere] * 2,
+        out_specs=(within, within),
         scratch_shapes=[
+            pltpu.VMEM((2, chans, 2, size_y, depth), jnp.bfloat16),
+            pltpu.VMEM((size_x + 4, 4 * chans, depth), jnp.bfloat16),
             pltpu.SemaphoreType.DMA((8,)),
             pltpu.SemaphoreType.DMA((8,)),
-            pltpu.SemaphoreType.DMA((9,)),
         ],
         compiler_params=pltpu.CompilerParams(collective_id=0, has_side_effects=True),
         name="halo",
-    )(
-        features, sides, jnp.zeros((chans, 2, size_y, depth), jnp.bfloat16),
-        jnp.zeros((size_x, 2 * chans, depth), jnp.bfloat16),
-    )
+    )(features, sides)
 
 
 def coarse_kernel(
@@ -496,8 +495,8 @@
 
 def local(features, w_first, w_second, w_lift, w_coarse, w_decode, w_joining):
     chans, size_x, size_y, depth = features.shape
-    own, rim = halo(features)
-    second, pooled = fine(own, rim, w_first, w_second, size_x)
+    beyond, rim = halo(features)
+    second, pooled = fine(features, beyond, rim, w_first, w_second)
     up = coarse_level(pooled, w_lift, w_coarse, w_decode, w_joining[:, chans:], size_y)
     return join(second, up, w_joining[:, :chans])
 

time: 144 us -> 78.1 us (0.54)
  Pallas kernels: 129 us -> 59.6 us
  local copies, waits for them, and re-layouts: 11.6 us -> 14.1 us
    pallas_call x1, Pallas kernels: 81.2 us -> 9.87 us  [halo(): pl.pallas_call(lambda *refs: halo_kernel(nx, ny, *refs), out_shape=(jax.S...]
    pallas_call x1, Pallas kernels: 16.5 us -> 21.4 us  [coarse_level(): pl.pallas_call(lambda *refs: coarse_kernel(nx, ny, *refs), out_shape=jax....]
    unnamed x38 -> x36, local copies, waits for them, and re-layouts: 5.86 us -> 8.5 us
    pallas_call x1, Pallas kernels: 28.4 us -> 25.8 us  [fine(): pl.pallas_call(fine_kernel, out_shape=(jax.ShapeDtypeStruct((size_x, rows...]
where the time goes in v3:
time: 78.1 us; the launch traced here: 77.5 us
  Pallas kernels  59.6 us (76%)
  local copies, waits for them, and re-layouts  14.1 us (18%)
  other arithmetic  3.58 us (5%)
    pallas_call x1, Pallas kernels, fine(): pl.pallas_call(fine_kernel, out_shape=(jax.ShapeDtypeStruct((size_x, rows...  25.8 us
    pallas_call x1, Pallas kernels, coarse_level(): pl.pallas_call(lambda *refs: coarse_kernel(nx, ny, *refs), out_shape=jax....  21.4 us
    pallas_call x1, Pallas kernels, halo(): pl.pallas_call(lambda *refs: halo_kernel(nx, ny, *refs), out_shape=(jax.S...  9.87 us
    unnamed x36, local copies, waits for them, and re-layouts  8.5 us
    transpose x3, local copies, waits for them, and re-layouts, side(): return jnp.transpose(v, (1, 2, 0, 3)).reshape(size_x, 2 * chans, depth)  2.74 us
    pallas_call x1, Pallas kernels, join(): pl.pallas_call(join_kernel, grid=(size_x // step,), out_shape=jax.ShapeDt...  2.55 us

profile of v3, /device:TPU:0, one launch (start us, length us, event | category | flops | bytes accessed | tf_op | source)
XLA Modules:
  0.0 77.5 jit_solution(9441207301626137363)
XLA Ops:
  0.0 0.0 copy-start
  0.0 0.1 add_convert_fusion
  0.1 0.1 broadcast_in_dim.7.edge_ref
  0.2 0.6 copy-done
  0.7 0.1 constant_dynamic-slice_fusion
  0.8 0.6 fusion
  1.4 1.4 %fusion.1 = (bf16[16,16]{1,0:T(8,128)(2,1)}, bf16[16,16]{1,0:T(8,128)(2,1)S(1)}) fusion(bf16[16,32]{1,0:T(8,128)(2,1)} %param.25), kind=kLoop, calls=%fused_computation.10 | loop fusion | bytes 2048 | tf_op jit(solution)/shard_map/slice | solution.py:501
  2.7 0.1 copy.35
  2.8 0.1 copy.34
  3.0 1.0 %copy.28 = bf16[27,16,16]{2,1,0:T(8,128)(2,1)S(1)} copy(bf16[27,16,16]{0,2,1:T(8,128)(2,1)} %param.20) | data formatting | bytes 27648 | tf_op args[1]
  4.0 0.1 copy.29
  4.1 0.1 reshape.43.w1_ref
  4.2 1.0 %copy.30 = bf16[27,16,16]{2,1,0:T(8,128)(2,1)S(1)} copy(bf16[27,16,16]{0,2,1:T(8,128)(2,1)} %param.21) | data formatting | bytes 27648 | tf_op args[2]
  5.2 0.1 copy.31
  5.3 0.1 reshape.45.w2_ref
  5.4 0.7 pad_convert_fusion.refs_1_
  6.1 1.2 %or_select_fusion.oy1 = s32[864,1]{1,0:T(8,128)S(1)} fusion(s32[864,1]{1,0:T(8,128)} %constant.51.clone, pred[864,1]{1,0:T(32,128)(4,1)} %constant.67, pred[864,1]{1,0:T(32,128)(4,1)} %constant.66, pred[]{:T(512)S(6)} %eq.14, pred[]{:T(512)S(6)} %eq.13), kind=kLoop, calls=%fused_computation.2 | loop fusion | flops 3456 | bytes 8642 | tf_op jit(solution)/shard_map/jit(_where)/select_n | solution.py:152
  7.3 2.1 %slice_bitcast_fusion.1 = (bf16[32,2,16,128]{3,1,0,2:T(2,128)(2,1)S(1)}, bf16[32,2,16,128]{3,1,0,2:T(2,128)(2,1)S(1)}) fusion(bf16[16,32,16,128]{3,2,1,0:T(8,128)(2,1)} %features_ref.1), kind=kLoop, calls=%fused_computation.4 | loop fusion | bytes 1048576 | tf_op jit(solution)/shard_map/transpose | solution.py:306
  9.5 0.3 copy.26
  9.8 0.0 copy-start.3
  9.8 0.0 copy-start.6
  9.8 0.0 copy-start.9
  9.8 0.0 copy-start.12
  9.8 0.0 copy-start.13
  9.9 0.3 copy.27
  10.2 0.8 %pad_maximum_fusion.refs_1_ = bf16[2,32,32,128]{3,2,1,0:T(8,128)(2,1)} fusion(bf16[1,32,32,128]{3,2,1,0:T(8,128)(2,1)S(1)} %bitcast.22, bf16[1,32,32,128]{3,2,1,0:T(8,128)(2,1)S(1)} %bitcast.21), kind=kLoop, calls=%fused_computation | loop fusion | flops 262144 | bytes 1048576 | tf_op jit(solution)/shard_map/stack | solution.py:308
  11.0 9.9 %halo.1 = (bf16[2,16,2,16,128]{4,3,2,1,0:T(8,128)(2,1)}, bf16[36,64,128]{2,1,0:T(8,128)(2,1)}) custom-call(bf16[16,32,16,128]{3,2,1,0:T(8,128)(2,1)} %features_ref.1, bf16[2,32,32,128]{3,2,1,0:T(8,128)(2,1)} %pad_maximum_fusion.refs_1_), custom_call_target="tpu_custom_call" | custom-call | tf_op jit(solution)/shard_map/halo/pallas_call | solution.py:311
  20.9 0.0 copy-done.3
  20.9 0.0 copy-done.6
  20.9 0.0 copy-done.9
  20.9 0.0 copy-done.12
  20.9 0.0 copy-done.13
  20.9 0.0 copy-start.4
  20.9 1.1 %copy-done.4 = bf16[36,64,128]{2,1,0:T(8,128)(2,1)S(1)} copy-done((bf16[36,64,128]{2,1,0:T(8,128)(2,1)S(1)}, bf16[36,64,128]{2,1,0:T(8,128)(2,1)}, u32[]{:S(2)}) %copy-start.4) | copy-done | bytes 589848
  22.0 0.0 copy-start.5
  22.0 0.9 %copy-done.5 = bf16[2,16,2,16,128]{4,3,2,1,0:T(8,128)(2,1)S(1)} copy-done((bf16[2,16,2,16,128]{4,3,2,1,0:T(8,128)(2,1)S(1)}, bf16[2,16,2,16,128]{4,3,2,1,0:T(8,128)(2,1)}, u32[]{:S(2)}) %copy-start.5) | copy-done | bytes 262168
  23.0 0.0 copy-start.7
  23.0 0.9 %copy-done.7 = bf16[864,48]{1,0:T(8,128)(2,1)S(1)} copy-done((bf16[864,48]{1,0:T(8,128)(2,1)S(1)}, bf16[864,48]{1,0:T(8,128)(2,1)}, u32[]{:S(2)}) %copy-start.7) | copy-done | bytes 82968
  23.9 0.0 copy-start.8
  23.9 0.9 %copy-done.8 = bf16[768,48]{1,0:T(8,128)(2,1)S(1)} copy-done((bf16[768,48]{1,0:T(8,128)(2,1)S(1)}, bf16[768,48]{1,0:T(8,128)(2,1)}, u32[]{:S(2)}) %copy-start.8) | copy-done | bytes 73752
  24.8 0.0 copy-start.10
  24.8 0.9 %copy-done.10 = bf16[48,960]{1,0:T(8,128)(2,1)S(1)} copy-done((bf16[48,960]{1,0:T(8,128)(2,1)S(1)}, bf16[48,960]{1,0:T(8,128)(2,1)}, u32[]{:S(2)}) %copy-start.10) | copy-done | bytes 92184
  25.7 0.0 copy-start.11
  25.7 0.9 %copy-done.11 = bf16[48,864]{1,0:T(8,128)(2,1)S(1)} copy-done((bf16[48,864]{1,0:T(8,128)(2,1)S(1)}, bf16[48,864]{1,0:T(8,128)(2,1)}, u32[]{:S(2)}) %copy-start.11) | copy-done | bytes 82968
  26.6 0.0 copy-start.1
  26.6 0.0 copy-start.2
  26.6 25.8 %fine.1 = (bf16[32,256,128]{2,1,0:T(8,128)(2,1)S(1)}, f32[2,8,128]{2,1,0:T(8,128)S(1)}) custom-call(bf16[16,32,16,128]{3,2,1,0:T(8,128)(2,1)} %features_ref.1, bf16[2,16,2,16,128]{4,3,2,1,0:T(8,128)(2,1)S(1)} %copy-done.5, bf16[36,64,128]{2,1,0:T(8,128)(2,1)S(1)} %copy-done.4, bf16[3,48,48]{2,1,0:T(8,128)(2,1)S(1)} %reshape.43.w1_ref, ...), custom_call_target="tpu_custom_call" | custom-call | flops 12655263744 | bytes 8000000 | tf_op jit(solution)/shard_map/fine/pallas_call | solution.py:167
  52.4 0.0 copy-start.14
  52.4 0.0 copy-start.15
  52.4 0.0 copy-done.1
  52.5 0.0 copy-done.2
  52.5 21.4 %coarse.1.up_ref = f32[2,256,128]{2,1,0:T(8,128)S(1)} custom-call(f32[2,8,128]{2,1,0:T(8,128)S(1)} %get-tuple-element.12.refs_0_, f32[128,512]{1,0:T(8,128)S(1)} %pad_convert_fusion.refs_1_, bf16[27,64,512]{2,1,0:T(8,128)(2,1)S(1)} %bitcast.20, bf16[64,128]{1,0:T(8,128)(2,1)S(1)} %pad.16.refs_3_, bf16[128,128]{1,0:T(8,128)(2,1)S(1)} %pad.17.refs_4_, ...), custom_call_target="tpu_custom_call" | custom-call | tf_op jit(solution)/shard_map/coarse/pallas_call | solution.py:473
  73.8 0.0 copy-done.14
  73.8 0.0 copy-done.15
  73.8 0.1 broadcast_multiply_fusion
  74.0 1.0 %mul.24.matrix_ref = bf16[256,256]{1,0:T(8,128)(2,1)S(1)} reshape(bf16[16,16,16,16]{3,2,1,0:T(8,128)(2,1)S(1)} %broadcast_multiply_fusion) | data formatting | bytes 262144 | tf_op jit(solution)/shard_map/mul | solution.py:209
  75.0 2.6 %join.1 = bf16[16,32,16,128]{3,2,1,0:T(8,128)(2,1)} custom-call(bf16[32,256,128]{2,1,0:T(8,128)(2,1)S(1)} %get-tuple-element.11.second_ref, f32[2,256,128]{2,1,0:T(8,128)S(1)} %coarse.1.up_ref, bf16[256,256]{1,0:T(8,128)(2,1)S(1)} %mul.24.matrix_ref), custom_call_target="tpu_custom_call" | custom-call | flops 536870912 | bytes 5000000 | tf_op jit(solution)/shard_map/join/pallas_call | solution.py:212
  (2 shorter events, 0.0 us)
Async XLA Ops:
  0.0 0.7 copy-start
  9.8 11.1 %copy-start.3 = (f32[8,128]{1,0:T(8,128)S(1)}, f32[8,128]{1,0:T(8,128)}, u32[]{:S(2)}) copy-start(f32[8,128]{1,0:T(8,128)} %constant.58.clone.lanes_ref.refs_6_) | copy-start | bytes 12292
  9.8 11.1 %copy-start.6 = (s32[768,1]{1,0:T(8,128)S(1)}, s32[768,1]{1,0:T(8,128)}, u32[]{:S(2)}) copy-start(s32[768,1]{1,0:T(8,128)} %constant.55.clone.oy2) | copy-start | bytes 9220
  9.8 11.1 %copy-start.9 = (f32[128,256]{1,0:T(8,128)S(1)}, f32[128,256]{1,0:T(8,128)}, u32[]{:S(2)}) copy-start(f32[128,256]{1,0:T(8,128)} %constant.57.clone.cells_ref) | copy-start | bytes 393220
  9.8 11.1 %copy-start.12 = (s32[1,960]{1,0:T(1,128)S(1)}, s32[1,960]{1,0:T(1,128)}, u32[]{:S(2)}) copy-start(s32[1,960]{1,0:T(1,128)} %constant.52.clone.iy1) | copy-start | bytes 11524
  9.8 11.1 %copy-start.13 = (s32[1,864]{1,0:T(1,128)S(1)}, s32[1,864]{1,0:T(1,128)}, u32[]{:S(2)}) copy-start(s32[1,864]{1,0:T(1,128)} %constant.56.clone.iy2) | copy-start | bytes 10372
  20.9 1.1 %copy-start.4 = (bf16[36,64,128]{2,1,0:T(8,128)(2,1)S(1)}, bf16[36,64,128]{2,1,0:T(8,128)(2,1)}, u32[]{:S(2)}) copy-start(bf16[36,64,128]{2,1,0:T(8,128)(2,1)} %get-tuple-element.10.rim_ref) | copy-start | bytes 1769476
  22.0 0.9 %copy-start.5 = (bf16[2,16,2,16,128]{4,3,2,1,0:T(8,128)(2,1)S(1)}, bf16[2,16,2,16,128]{4,3,2,1,0:T(8,128)(2,1)}, u32[]{:S(2)}) copy-start(bf16[2,16,2,16,128]{4,3,2,1,0:T(8,128)(2,1)} %get-tuple-element.9.beyond_ref) | copy-start | bytes 786436
  23.0 0.9 %copy-start.7 = (bf16[864,48]{1,0:T(8,128)(2,1)S(1)}, bf16[864,48]{1,0:T(8,128)(2,1)}, u32[]{:S(2)}) copy-start(bf16[864,48]{1,0:T(8,128)(2,1)} %constant.49.clone.l1) | copy-start | bytes 248836
  23.9 0.9 %copy-start.8 = (bf16[768,48]{1,0:T(8,128)(2,1)S(1)}, bf16[768,48]{1,0:T(8,128)(2,1)}, u32[]{:S(2)}) copy-start(bf16[768,48]{1,0:T(8,128)(2,1)} %constant.53.clone.l2) | copy-start | bytes 221188
  24.8 0.9 %copy-start.10 = (bf16[48,960]{1,0:T(8,128)(2,1)S(1)}, bf16[48,960]{1,0:T(8,128)(2,1)}, u32[]{:S(2)}) copy-start(bf16[48,960]{1,0:T(8,128)(2,1)} %constant.50.clone.r1) | copy-start | bytes 276484
  25.7 0.9 %copy-start.11 = (bf16[48,864]{1,0:T(8,128)(2,1)S(1)}, bf16[48,864]{1,0:T(8,128)(2,1)}, u32[]{:S(2)}) copy-start(bf16[48,864]{1,0:T(8,128)(2,1)} %constant.54.clone.r2) | copy-start | bytes 248836
  26.6 25.8 %copy-start.1 = (bf16[64,27,512]{2,0,1:T(8,128)(2,1)S(1)}, bf16[64,27,512]{2,0,1:T(8,128)(2,1)}, u32[]{:S(2)}) copy-start(bf16[64,27,512]{2,0,1:T(8,128)(2,1)} %param.23) | copy-start | bytes 5308420
  26.6 25.9 %copy-start.2 = (f32[256,128]{1,0:T(8,128)S(1)}, f32[256,128]{1,0:T(8,128)}, u32[]{:S(2)}) copy-start(f32[256,128]{1,0:T(8,128)} %constant.59.clone.refs_5_) | copy-start | bytes 393220
  52.4 21.4 %copy-start.14 = (bf16[16,16]{1,0:T(8,128)(2,1)S(1)}, bf16[16,16]{1,0:T(8,128)(2,1)}, u32[]{:S(2)}) copy-start(bf16[16,16]{1,0:T(8,128)(2,1)} %fusion) | copy-start | bytes 1540
  52.4 21.4 %copy-start.15 = (bf16[16,16]{1,0:T(8,128)(2,1)S(1)}, bf16[16,16]{1,0:T(8,128)(2,1)}, u32[]{:S(2)}) copy-start(bf16[16,16]{1,0:T(8,128)(2,1)} %get-tuple-element.15) | copy-start | bytes 1540
